TPU v7x, 32 devices: a whole 2x2x4 slice. The times are simulated.
32 devices in a mesh: parts: 2 (over y), row: 4 (over z), col: 4 (over x, core).
Axes of the slice: x: 2, y: 2, z: 4, core: 2. Of those that a mesh axis runs over, the one named last changes fastest.
Arguments:
- amplitudes: bfloat16 [8, 100, 512, 512], P('parts', 'col', 'row'), parts along dimension 0, may hold values from -12 to 12
- integrals: bfloat16 [200, 512, 512], P(('parts', 'col'), 'row'), parts along dimension 0, may hold values from -0.109375 to 0.109375
- occ_irrep: int32 [200], P('parts'), parts along dimension 0, may hold values from 0 to 7, as said below
- vir_irrep: int32 [1024], P('parts'), parts along dimension 0, may hold values from 0 to 7, as said below
- screen: int32 [200, 8], P('parts'), parts along dimension 0, may hold values 0 or 1
- occ_energy: float32 [200], P('parts'), parts along dimension 0, may hold values from -1 to -0.3
- vir_energy: float32 [1024], P('parts'), parts along dimension 0, may hold values from 0.1 to 1
Outputs:
- update: float32 [512, 8, 512], P('row', 'parts', 'col'), parts along dimension 1
There are 2 independent parts, one for each index of `parts`. A program takes and returns all parts, laid end to end along the dimension named above; each array names one. Nothing has to cross between parts.
Inputs may be any that keep to these rules, and one draw needn't show every extreme that they name: `occ_irrep`: the labels never fall from one orbital to the next; the first is 0 and the last is 7. `vir_irrep`: the labels never fall from one orbital to the next and every label from 0 to 7 occurs; exactly one label covers 256 virtual orbitals, every other label fewer.
All inputs are finite; a program needn't handle non-finite values.
Results may differ from a plain program's by a relative error of at most 0.0003.
Values may be sent and summed in bfloat16 or wider, within the bound.
No kernel may reach another device: no remote copies, remote signals or barrier semaphores. Data moves between devices by JAX's collectives and lax.ppermute only.
A program may use at most 128 MiB of HBM per device.

v0:
```python
import jax
import jax.numpy as jnp
from jax import lax
from jax.experimental import pallas as pl
from jax.experimental.pallas import tpu as pltpu
from jax.sharding import PartitionSpec as P

FOLD = 256
K_STEP = 5


def folded_integrals(integrals, occ_local, vir_local, vir_irrep, pair_label, screen_rows):
    irrep_codes = jnp.arange(8, dtype=jnp.int32)
    screen_local = jnp.sum(
        screen_rows[:, None, :] * (vir_local[None, :, None] == irrep_codes).astype(jnp.int32),
        axis=2,
    )
    target = jnp.bitwise_xor(
        jnp.bitwise_xor(occ_local[:, None], vir_local[None, :]), pair_label
    )
    target = jnp.where(screen_local == 1, target, -1)
    keep = target[:, :, None] == vir_irrep[None, None, :]
    kept = jnp.where(keep, integrals, jnp.zeros_like(integrals))
    return kept[:, :, :FOLD] + kept[:, :, FOLD:]


NARROW = 64
CAPS = (22, 3)
FEW_CAPS = (4, 10)
FEW_WIDE = 5


def largest_irrep(vir_ref):
    return jnp.where(vir_ref[0] == vir_ref[FOLD - 1], vir_ref[0], vir_ref[FOLD])


def label_columns(row_labels):
    return jnp.transpose(jnp.broadcast_to(row_labels, (8, row_labels.shape[1])))


def as_bf16(labels):
    return labels.astype(jnp.float32).astype(jnp.bfloat16)


def label_mix(mix_ref, column_ref, row_ref, row, big, keep_big):
    depth = mix_ref.shape[0]
    column_ref[...] = label_columns(row_ref[...])
    column = column_ref[pl.ds(pl.multiple_of(row * depth, depth), depth), :1]
    is_big = row_ref[...] == big
    wanted = is_big if keep_big else jnp.logical_not(is_big)
    mix_ref[...] = as_bf16(jnp.where(wanted, jnp.bitwise_xor(column, row_ref[...]), 8))


def kept_folded(int_ref, mix_ref, j, x):
    tile = int_ref[j]
    wanted = as_bf16(jnp.full(mix_ref.shape, x))
    kept = jnp.where(mix_ref[...] == wanted, tile, jnp.zeros_like(tile))
    return kept[:, :FOLD] + kept[:, FOLD:]


def narrow_fold(kept, bits, local):
    half = kept.shape[0] // 2
    lane = lax.broadcasted_iota(jnp.int32, (half, 2 * NARROW), 1)
    narrow = (kept[:, : 2 * NARROW] + kept[:, 2 * NARROW:]).astype(jnp.float32)
    narrow = narrow + pltpu.roll(narrow, NARROW, 1)
    on = jnp.bitwise_and(lax.shift_right_logical(jnp.full(local.shape, bits), local), 1) == 1
    narrow = jnp.where(on, narrow, 0.0)
    return jnp.where(lane < NARROW, narrow[:half], narrow[half:]).astype(jnp.bfloat16)


def screen_bits(screen_ref, k):
    bits = screen_ref[0, k]
    for g in range(1, 8):
        bits = bits + screen_ref[g, k] * (1 << g)
    return bits


def wide_kernel(
    occ_ref, vir_ref, screen_ref, place_ref, int_ref, row_ref,
    few_ref, m2a_ref, m2b_ref, m3a_ref, m3b_ref, pos2_ref, pos3_ref, posx_ref, form_ref, count_ref,
    mix_ref, small_mix_ref, column_ref, counts_ref, batch,
):
    step = pl.program_id(0)
    k_step, depth, total = int_ref.shape
    half = depth // 2
    row, col = place_ref[0], place_ref[1]
    pair_label = occ_ref[batch]
    big = largest_irrep(vir_ref)
    k_all = k_step * pl.num_programs(0)
    mostly_zero = (occ_ref[col * k_all] == pair_label) | (occ_ref[(col + 1) * k_all - 1] == pair_label)
    most = FEW_CAPS[-1]

    @pl.when(step == 0)
    def _():
        for n in range(3):
            counts_ref[n] = 0
        label_mix(mix_ref, column_ref, row_ref, row, big, True)

        @pl.when(mostly_zero)
        def _():
            label_mix(small_mix_ref, column_ref, row_ref, row, big, False)

    local = column_ref[pl.ds(pl.multiple_of(row * depth, depth), depth), :1]

    @pl.loop(0, k_step)
    def _(j):
        k = step * k_step + j
        k_whole = col * k_all + k
        x = jnp.bitwise_xor(occ_ref[k_whole], pair_label)
        on_big = screen_ref[jnp.bitwise_xor(big, x), k_whole] == 1
        actives = (on_big & (x != 0), on_big & (x == 0), x != 0)
        pos2, pos3, posx = [jnp.where(active, counts_ref[n], -1) for n, active in enumerate(actives)]
        for n, active in enumerate(actives):
            counts_ref[n] = counts_ref[n] + active.astype(jnp.int32)
        pos2_ref[k], pos3_ref[k], posx_ref[k] = pos2, pos3, posx

        @pl.when(pos2 >= 0)
        def _():
            wide = kept_folded(int_ref, mix_ref, j, x)
            short = wide[:half] + wide[half:]

            @pl.when(mostly_zero & (pos2 < most))
            def _():
                for piece in range(2):
                    few_ref[pos2, 1 + piece] = short[:, piece * 2 * NARROW:(piece + 1) * 2 * NARROW]

            @pl.when(pos2 < CAPS[0])
            def _():
                m2a_ref[pos2] = short

            @pl.when(pos2 >= CAPS[0])
            def _():
                m2b_ref[pos2 - CAPS[0]] = short

        @pl.when(mostly_zero & (posx >= 0) & (posx < most))
        def _():
            kept = kept_folded(int_ref, small_mix_ref, j, x)
            few_ref[posx, 0] = narrow_fold(kept, screen_bits(screen_ref, k_whole), local)

        @pl.when(pos3 >= 0)
        def _():
            wide = kept_folded(int_ref, mix_ref, j, x)

            @pl.when(pos3 < CAPS[0])
            def _():
                m3a_ref[pos3] = wide

            @pl.when(pos3 >= CAPS[0])
            def _():
                m3b_ref[pos3 - CAPS[0]] = wide

    @pl.when(step == pl.num_programs(0) - 1)
    def _():
        labels = row_ref[...]
        lanes = lax.broadcasted_iota(jnp.int32, labels.shape, 1)
        ahead = pltpu.roll(labels, total - NARROW, 1)
        long = (labels == ahead) & (lanes < total - NARROW) & (labels != big)
        too_long = jnp.max(long.astype(jnp.int32)) == 1
        n2, n3, nx = counts_ref[0], counts_ref[1], counts_ref[2]
        count_ref[0] = nx
        one_label = occ_ref[0] == pair_label
        form = jnp.where((nx <= FEW_CAPS[0]) & (n3 <= CAPS[0]), 3, jnp.where(nx <= FEW_CAPS[1], 4, 5))
        form = jnp.where(mostly_zero, form, 5)
        form = jnp.where((n3 <= FEW_WIDE) & (n2 <= CAPS[0]), 2, form)
        form = jnp.where(one_label, form, 6)
        form = jnp.where(n3 == 0, jnp.where(n2 <= CAPS[0], 0, 1), form)
        form_ref[0] = jnp.where(too_long, 6, form)


def wide_blocks(integrals, occ_irrep, vir_irrep, screen, place, batch):
    occ_share, depth, total = integrals.shape
    shapes = [(n, depth // 2, FOLD) for n in CAPS] + [(n, depth, FOLD) for n in CAPS]
    few = (FEW_CAPS[-1], 3, depth // 2, 2 * NARROW)
    smem = pl.BlockSpec(memory_space=pltpu.SMEM)

    def kernel(*refs):
        wide_kernel(*refs, batch)

    return pl.pallas_call(
        kernel,
        grid_spec=pltpu.PrefetchScalarGridSpec(
            num_scalar_prefetch=4,
            grid=(occ_share // K_STEP,),
            in_specs=[
                pl.BlockSpec((K_STEP, depth, total), lambda k, *_: (k, 0, 0)),
                pl.BlockSpec((1, total), lambda k, *_: (0, 0)),
            ],
            out_specs=[pl.BlockSpec(few, lambda k, *_: (0, 0, 0, 0))]
            + [pl.BlockSpec(v, lambda k, *_: (0, 0, 0)) for v in shapes]
            + [smem] * 5,
            scratch_shapes=[
                pltpu.VMEM((depth, total), jnp.bfloat16),
                pltpu.VMEM((depth, total), jnp.bfloat16),
                pltpu.VMEM((total, 8), jnp.int32),
                pltpu.SMEM((3,), jnp.int32),
            ],
        ),
        out_shape=[jax.ShapeDtypeStruct(v, jnp.bfloat16) for v in [few] + shapes]
        + [jax.ShapeDtypeStruct((n,), jnp.int32) for n in (occ_share, occ_share, occ_share, 1, 1)],
        cost_estimate=cost(5),
        compiler_params=pltpu.CompilerParams(vmem_limit_bytes=24 * 1024 * 1024),
    )(occ_irrep, vir_irrep, screen.T, place, integrals, vir_irrep[None, :])


def narrow_kernel(
    occ_ref, vir_ref, screen_ref, place_ref, int_ref, row_ref, few_ref, narrow_ref, mix_ref, column_ref, batch,
):
    step = pl.program_id(0)
    k_step, depth, total = int_ref.shape
    row, col = place_ref[0], place_ref[1]

    @pl.when(step == 0)
    def _():
        label_mix(mix_ref, column_ref, row_ref, row, largest_irrep(vir_ref), False)
        if few_ref is not None:
            for n in range(few_ref.shape[0]):
                for piece in range(2):
                    narrow_ref[k_step * pl.num_programs(0) + 2 * n + piece] = few_ref[n, 1 + piece]

    local = column_ref[pl.ds(pl.multiple_of(row * depth, depth), depth), :1]
    for j in range(k_step):
        k_whole = (col * pl.num_programs(0) + step) * k_step + j
        x = jnp.bitwise_xor(occ_ref[k_whole], occ_ref[batch])
        kept = kept_folded(int_ref, mix_ref, j, x)
        narrow_ref[step * k_step + j] = narrow_fold(kept, screen_bits(screen_ref, k_whole), local)


def narrow_blocks(integrals, occ_irrep, vir_irrep, screen, place, few, batch):
    occ_share, depth, total = integrals.shape
    extra = [] if few is None else [few]
    count = occ_share + sum(2 * v.shape[0] for v in extra)
    shape = (count, depth // 2, 2 * NARROW)

    def kernel(*refs):
        narrow_kernel(*(refs if extra else refs[:6] + (None,) + refs[6:]), batch)

    return pl.pallas_call(
        kernel,
        grid_spec=pltpu.PrefetchScalarGridSpec(
            num_scalar_prefetch=4,
            grid=(occ_share // K_STEP,),
            in_specs=[
                pl.BlockSpec((K_STEP, depth, total), lambda k, *_: (k, 0, 0)),
                pl.BlockSpec((1, total), lambda k, *_: (0, 0)),
            ] + [pl.BlockSpec(v.shape, lambda k, *_: (0, 0, 0, 0)) for v in extra],
            out_specs=pl.BlockSpec(shape, lambda k, *_: (0, 0, 0)),
            scratch_shapes=[pltpu.VMEM((depth, total), jnp.bfloat16), pltpu.VMEM((total, 8), jnp.int32)],
        ),
        out_shape=jax.ShapeDtypeStruct(shape, jnp.bfloat16),
        cost_estimate=cost(5),
        compiler_params=pltpu.CompilerParams(vmem_limit_bytes=16 * 1024 * 1024),
    )(occ_irrep, vir_irrep, screen.T, place, integrals, vir_irrep[None, :], *extra)


def cost(micros):
    return pl.CostEstimate(flops=int(micros * 1e9), bytes_accessed=int(micros * 3e6), transcendentals=0)


SLOTS = (0, 1, 3, 2)
NEAR = 3


def amplitude_rows(column_ref, row_ref, occ_ref, row, batch, share):
    column_ref[...] = label_columns(row_ref[...])
    column = column_ref[pl.ds(pl.multiple_of(row * share, share), share), :1]
    return jnp.concatenate([jnp.bitwise_xor(column, occ_ref[i]) for i in range(batch)], axis=0)


def write_quarters(total_ref, col, outs):
    rows, fold = total_ref.shape
    width, height = fold // 2, rows // 2
    for t, out_ref in enumerate(outs):
        goal = jnp.bitwise_xor(col, t)
        lanes = pl.ds(pl.multiple_of((goal % 2) * width, width), width)
        lines = pl.ds(pl.multiple_of((goal // 2) * height, height), height)
        out_ref[...] = total_ref[lines, lanes].reshape(out_ref.shape)


def chosen(refs, starts, pos, pick):
    block = None
    for n, group in enumerate(refs):
        inside = (pos >= starts[n]) & (pos < starts[n + 1])
        at = jnp.clip(pos - starts[n], 0, starts[n + 1] - starts[n] - 1)
        found = pick(group, at)
        found = jnp.where(inside, found, jnp.zeros_like(found))
        block = found if block is None else block + found
    return block


def starts_of(arrays):
    starts = [0]
    for v in arrays:
        starts.append(starts[-1] + v.shape[0])
    return starts


def mask_kernel(
    occ_ref, place_ref, posx_ref, amp_ref, row_ref, lhs_ref, far_ref, fold_ref, few_lhs_ref,
    mix_ref, column_ref, amp_buffer, sems,
):
    batch, k_all, share, total = amp_ref.shape
    rows, groups = batch * share, k_all // K_STEP
    row, col = place_ref[0], place_ref[1]

    def fetch(group):
        slot = group % 2
        source = amp_ref.at[:, pl.ds(group * K_STEP, K_STEP)]
        return pltpu.make_async_copy(source, amp_buffer.at[slot], sems.at[slot])

    fetch(0).start()
    column = amplitude_rows(column_ref, row_ref, occ_ref, row, batch, share)
    mix_ref[...] = as_bf16(jnp.bitwise_xor(column, row_ref[...]))
    if few_lhs_ref is not None:
        few_lhs_ref[...] = jnp.zeros(few_lhs_ref.shape, jnp.bfloat16)

    @pl.loop(0, groups)
    def _(group):
        slot = group % 2

        @pl.when(group + 1 < groups)
        def _():
            fetch(group + 1).start()

        fetch(group).wait()

        @pl.loop(0, K_STEP)
        def _(j):
            wanted = as_bf16(jnp.full((rows, share), occ_ref[col * k_all + group * K_STEP + j]))
            folded = None
            for n, s in enumerate(SLOTS):
                place = pl.ds(pl.multiple_of(jnp.bitwise_xor(row, s) * share, share), share)
                tile = amp_buffer[slot, :, j, :, place].reshape(rows, share)
                piece = jnp.where(mix_ref[:, place] == wanted, tile, jnp.zeros_like(tile))
                if n < NEAR:
                    lhs_ref[group, :, pl.ds(pl.multiple_of((n * K_STEP + j) * share, share), share)] = piece
                else:
                    far_ref[group, :, pl.ds(pl.multiple_of(j * share, share), share)] = piece
                folded = piece if folded is None else folded + piece
            fold_ref[group, :, pl.ds(pl.multiple_of(j * share, share), share)] = folded
            if few_lhs_ref is not None:
                posx = posx_ref[group * K_STEP + j]

                @pl.when((posx >= 0) & (posx < few_lhs_ref.shape[0]))
                def _():
                    third = lhs_ref[group, :, pl.ds(pl.multiple_of((2 * K_STEP + j) * share, share), share)]
                    few_lhs_ref[posx, 0] = third
                    few_lhs_ref[posx, 1] = far_ref[group, :, pl.ds(pl.multiple_of(j * share, share), share)]


def masked_amplitudes(amplitudes, occ_irrep, vir_irrep, place, posx, few):
    batch, k_all, share, total = amplitudes.shape
    rows, groups = batch * share, k_all // K_STEP
    smem = pl.BlockSpec(memory_space=pltpu.SMEM)
    vmem = pl.BlockSpec(memory_space=pltpu.VMEM)
    hbm = pl.BlockSpec(memory_space=pltpu.HBM)
    shapes = [(groups, rows, w) for w in (NEAR * K_STEP * share, K_STEP * share, K_STEP * share)]
    shapes += [(few, 2, rows, share)] if few else []

    def kernel(*refs):
        mask_kernel(*(refs if few else refs[:8] + (None,) + refs[8:]))

    return pl.pallas_call(
        kernel,
        in_specs=[smem, smem, smem, hbm, vmem],
        out_specs=[vmem] * len(shapes),
        out_shape=[jax.ShapeDtypeStruct(v, jnp.bfloat16) for v in shapes],
        scratch_shapes=[
            pltpu.VMEM((rows, total), jnp.bfloat16),
            pltpu.VMEM((total, 8), jnp.int32),
            pltpu.VMEM((2, batch, K_STEP, share, total), jnp.bfloat16),
            pltpu.SemaphoreType.DMA((2,)),
        ],
        cost_estimate=cost(7),
        compiler_params=pltpu.CompilerParams(vmem_limit_bytes=28 * 1024 * 1024),
    )(occ_irrep, place, posx, amplitudes, vir_irrep[None, :])


def make_first_kernel(few, n3, starts3):
    def kernel(pos3_ref, posx_ref, place_ref, lhs_ref, far_ref, *refs):
        sources = 3 if few else 6
        narrow_refs, refs = refs[:sources], refs[sources:]
        m3_refs = [refs[3 * n:3 * n + 3] for n in range(n3)]
        narrow_sum, wide_sum, narrow_rhs, wide_rhs = refs[3 * n3:]
        row = place_ref[0]
        at_end = (row == 0) | (row == 3)
        groups, _, depth = lhs_ref.shape
        share = depth // (NEAR * K_STEP)
        half = share // 2
        lane = lax.broadcasted_iota(jnp.int32, (half, 2 * NARROW), 1)

        narrow_sum[...] = jnp.zeros(narrow_sum.shape, jnp.float32)
        wide_sum[...] = jnp.zeros(wide_sum.shape, jnp.float32)

        @pl.loop(0, groups)
        def _(group):
            @pl.loop(0, K_STEP)
            def _(j):
                k = group * K_STEP + j
                if few:
                    blocks = [ref[k] for ref in narrow_refs]
                else:
                    own, e1, o1, e2, o2, e3 = [ref[k] for ref in narrow_refs]
                    blocks = (own, e1, jnp.where(at_end, e3, o1), jnp.where(at_end, e2, o2))
                for n, block in enumerate(blocks):
                    zero = jnp.zeros_like(block)
                    first = pl.multiple_of((n * K_STEP + j) * share, share)
                    narrow_rhs[pl.ds(first, half)] = jnp.where(lane < NARROW, block, zero)
                    narrow_rhs[pl.ds(first + half, half)] = jnp.where(lane < NARROW, zero, block)
                for n in range(3 if n3 else 0):
                    block = chosen(m3_refs, starts3, pos3_ref[k], lambda group, at, n=n: group[n][at])
                    if n == 2:
                        block = jnp.where(at_end, jnp.zeros_like(block), block)
                    wide_rhs[pl.ds(pl.multiple_of((n * K_STEP + j) * share, share), share)] = block

            narrow = jnp.dot(lhs_ref[group], narrow_rhs[:depth], preferred_element_type=jnp.float32)
            if not few:
                narrow += jnp.dot(far_ref[group], narrow_rhs[depth:], preferred_element_type=jnp.float32)
            narrow_sum[...] += narrow
            if n3:
                wide_sum[...] += jnp.dot(lhs_ref[group], wide_rhs[...], preferred_element_type=jnp.float32)

    return kernel


def first_product(lhs, far_lhs, pos3, posx, place, narrow, few, m3):
    groups, rows, depth = lhs.shape
    vmem = pl.BlockSpec(memory_space=pltpu.VMEM)
    smem = pl.BlockSpec(memory_space=pltpu.SMEM)
    arrays = list(narrow) + [v for group in m3 for v in group]
    wide = (rows, FOLD) if m3 else (16, FOLD)
    wide_depth = depth if m3 else 16
    return pl.pallas_call(
        make_first_kernel(few, len(m3), starts_of([v[0] for v in m3])),
        in_specs=[smem] * 3 + [vmem] * (2 + len(arrays)),
        out_specs=[vmem] * 2,
        out_shape=[jax.ShapeDtypeStruct(v, jnp.float32) for v in ((rows, 2 * NARROW), wide)],
        scratch_shapes=[
            pltpu.VMEM((depth // NEAR * len(SLOTS), 2 * NARROW), jnp.bfloat16),
            pltpu.VMEM((wide_depth, FOLD), jnp.bfloat16),
        ],
        cost_estimate=cost(9 if m3 else 6),
        compiler_params=pltpu.CompilerParams(vmem_limit_bytes=32 * 1024 * 1024),
    )(pos3, posx, place, lhs, far_lhs, *arrays)


def make_last_kernel(few, n2, starts2, n3, starts3):
    def kernel(
        occ_ref, vir_ref, pos2_ref, pos3_ref, count_ref, place_ref, fold_ref, far_ref, row_ref, narrow_ref, wide_ref,
        *refs
    ):
        m2_refs, refs = refs[:n2], refs[n2:]
        m3_refs = [refs[2 * n:2 * n + 2] for n in range(n3)]
        refs = refs[2 * n3:]
        outs = refs[:4]
        column_ref, total_ref, short_rhs, far_rhs = refs[4:]
        row, col = place_ref[0], place_ref[1]
        at_end = (row == 0) | (row == 3)
        groups, rows, width = fold_ref.shape
        share = width // K_STEP
        batch = rows // share
        @pl.loop(0, groups * K_STEP)
        def _(k):
            here = pl.ds(pl.multiple_of(k * share, share), share)
            if few:
                pos2 = pos2_ref[k]
                at = jnp.maximum(pos2, 0)
                own, e1, o1, two, three, _ = m2_refs
                pieces = []
                for piece in range(2):
                    close = groups * K_STEP + 2 * at + piece
                    block = own[at, 1 + piece] + e1[close] + two[at, 1 + piece]
                    block = block + jnp.where(at_end, three[at, 1 + piece], o1[close])
                    pieces.append(jnp.where(pos2 >= 0, block, jnp.zeros_like(block)))
                short = jnp.concatenate(pieces, axis=1)
            else:
                short = chosen(m2_refs, starts2, pos2_ref[k], lambda ref, at: ref[at])
            short_rhs[here] = jnp.concatenate([short, short], axis=0)
            if n3:
                far_rhs[here] = chosen(
                    m3_refs, starts3, pos3_ref[k], lambda pair, at: jnp.where(at_end, pair[0][at], pair[1][at])
                )

        column = amplitude_rows(column_ref, row_ref, occ_ref, row, batch, share)
        target = jnp.bitwise_xor(column, occ_ref[batch])
        both = narrow_ref[...]
        if few:
            two, three, few_lhs_ref = m2_refs[3:]
            half = share // 2
            lane = lax.broadcasted_iota(jnp.int32, (half, 2 * NARROW), 1)
            for n in range(few_lhs_ref.shape[0]):
                used = n < count_ref[0]
                for slot, wanted, ref in ((0, used & at_end, three), (1, used, two)):
                    block = ref[n, 0]
                    zero = jnp.zeros_like(block)
                    block = jnp.where(wanted, block, zero)
                    rhs = jnp.concatenate(
                        [jnp.where(lane < NARROW, block, zero), jnp.where(lane < NARROW, zero, block)], axis=0
                    )
                    both += jnp.dot(few_lhs_ref[n, slot], rhs, preferred_element_type=jnp.float32)
        both = both + pltpu.roll(both, NARROW, 1)
        both = jnp.concatenate([both] * (FOLD // (2 * NARROW)), axis=1)
        part = wide_ref[...] if n3 else 0.0
        for group in range(groups):
            here = pl.ds(group * width, width)
            part += jnp.dot(fold_ref[group], short_rhs[here], preferred_element_type=jnp.float32)
            if n3:
                part += jnp.dot(far_ref[group], far_rhs[here], preferred_element_type=jnp.float32)
        total_ref[...] = jnp.where(target == largest_irrep(vir_ref), part, both)
        write_quarters(total_ref, col, outs)

    return kernel


def last_product(far_lhs, fold, occ_irrep, vir_irrep, pos2, pos3, count, place, narrow_sum, wide_sum, few, m2, m3, batch):
    groups, rows, width = fold.shape
    share = rows // batch
    vmem = pl.BlockSpec(memory_space=pltpu.VMEM)
    smem = pl.BlockSpec(memory_space=pltpu.SMEM)
    arrays = [narrow_sum, wide_sum] + list(m2) + [v for group in m3 for v in group]
    quarter = (batch // 2, share, FOLD // 2)
    whole = groups * width
    far_lhs = far_lhs if m3 else jnp.zeros((8, 128), jnp.bfloat16)
    return pl.pallas_call(
        make_last_kernel(few, len(m2), starts_of(m2), len(m3), starts_of([v[0] for v in m3])),
        in_specs=[smem] * 6 + [vmem] * (3 + len(arrays)),
        out_specs=[vmem] * 4,
        out_shape=[jax.ShapeDtypeStruct(quarter, jnp.float32)] * 4,
        scratch_shapes=[
            pltpu.VMEM((vir_irrep.shape[0], 8), jnp.int32),
            pltpu.VMEM((rows, FOLD), jnp.float32),
            pltpu.VMEM((whole, FOLD), jnp.bfloat16),
            pltpu.VMEM((whole if m3 else 16, FOLD), jnp.bfloat16),
        ],
        cost_estimate=cost(4 if m3 else 2),
        compiler_params=pltpu.CompilerParams(vmem_limit_bytes=32 * 1024 * 1024),
    )(occ_irrep, vir_irrep, pos2, pos3, count, place, fold, far_lhs, vir_irrep[None, :], *arrays)


def dense_product(amplitudes, whole, occ_irrep, occ_local, vir_local, vir_irrep):
    batch = amplitudes.shape[0]
    keep = (
        jnp.bitwise_xor(occ_irrep[:batch, None], occ_local[None, :])[:, :, None, None]
        == jnp.bitwise_xor(vir_local[:, None], vir_irrep[None, :])[None, None]
    )
    kept = jnp.where(keep, amplitudes, jnp.zeros_like(amplitudes))
    return lax.dot_general(
        kept, whole, (((1, 3), (0, 1)), ((), ())), preferred_element_type=jnp.float32
    )


def finish(cycle, occ_irrep, vir_irrep, occ_energy, vir_energy, a_start, a_size, b_start, b_size, batch):
    label_a = lax.dynamic_slice_in_dim(vir_irrep, a_start, a_size)
    label_b = lax.dynamic_slice_in_dim(vir_irrep, b_start, b_size)
    energy_a = lax.dynamic_slice_in_dim(vir_energy, a_start, a_size)
    energy_b = lax.dynamic_slice_in_dim(vir_energy, b_start, b_size)
    target = jnp.bitwise_xor(
        jnp.bitwise_xor(occ_irrep[:batch, None], occ_irrep[batch]), label_a[None, :]
    )
    keep = label_b[:, None, None] == target[None, :, :]
    denominator = (
        occ_energy[:batch][None, :, None]
        + occ_energy[batch]
        - energy_a[None, None, :]
        - energy_b[:, None, None]
    )
    swapped = jnp.transpose(cycle, (2, 0, 1))
    return jnp.where(keep, swapped, 0.0) / denominator


def on_square(amplitudes, integrals, occ_irrep, vir_irrep, screen):
    batch, occ_share, share, vir_total = amplitudes.shape
    row = lax.axis_index("row")
    col = lax.axis_index("col")
    place = jnp.stack([row, col]).astype(jnp.int32)
    few, m2a, m2b, m3a, m3b, pos2, pos3, posx, form, count = wide_blocks(
        integrals, occ_irrep, vir_irrep, screen, place, batch
    )
    outer = [(0, 1), (1, 0), (2, 3), (3, 2)]
    inner = [(1, 2), (2, 1)]
    inward = [(0, 1), (3, 2)]
    outward = [(1, 0), (2, 3)]
    ends = [(0, 3), (3, 0)]
    second = [(r, r ^ 2) for r in range(4)]

    def move(v, pairs):
        return lax.ppermute(v, "row", pairs)

    def sparse(use_few, choose):
        def run(few, m2a, m2b, m3a, m3b):
            shorts, wides = choose(m2a, m2b, m3a, m3b)
            near = [(own, move(own, outer), move(own, inner)) for own in wides]
            few = few[:use_few] if use_few else None
            narrow = narrow_blocks(integrals, occ_irrep, vir_irrep, screen, place, few, batch)
            if use_few:
                e1, o1 = move(narrow, outer), move(narrow, inner)
                lhs, far_lhs, fold, few_lhs = masked_amplitudes(
                    amplitudes, occ_irrep, vir_irrep, place, posx, use_few
                )
                near, e1, o1, few, _ = lax.optimization_barrier((near, e1, o1, few, fold))
                two, three = move(few, second), move(few, ends)
                blocks = (narrow, e1, o1)
                sums = (few, e1, o1, two, three, few_lhs)
            else:
                h1 = [move(v, inward) for v in shorts]
                o1, e1 = move(narrow, inner), move(narrow, outward)
                lhs, far_lhs, fold = masked_amplitudes(amplitudes, occ_irrep, vir_irrep, place, posx, 0)
                near, h1, o1, e1, _ = lax.optimization_barrier((near, h1, o1, e1, fold))
                h2 = [move(own + v, inner) for own, v in zip(shorts, h1)]
                e1 = e1 + move(narrow, inward)
                e2 = move(o1, outward)
                h2, e1, e2 = lax.optimization_barrier((h2, e1, e2))
                h3 = [move(own + v, outward) for own, v in zip(shorts, h2)]
                o2 = move(e1, inner)
                blocks = (narrow, e1, o1, e2, o2, move(o2, outward))
                sums = [a + b + c + d for a, b, c, d in zip(shorts, h1, h2, h3)]
            far = [(move(o, outward), move(e, inner)) for _, e, o in near]
            narrow_sum, wide_sum = first_product(
                lhs, far_lhs, pos3, posx, place, blocks, bool(use_few), near
            )
            return list(last_product(
                far_lhs, fold, occ_irrep, vir_irrep, pos2, pos3, count, place, narrow_sum, wide_sum, bool(use_few), sums,
                far, batch
            ))

        return run

    def dense(*_):
        occ_local = lax.dynamic_slice_in_dim(occ_irrep, col * occ_share, occ_share)
        vir_local = lax.dynamic_slice_in_dim(vir_irrep, row * share, share)
        screen_rows = lax.dynamic_slice_in_dim(screen, col * occ_share, occ_share, 0)
        fold = folded_integrals(
            integrals, occ_local, vir_local, vir_irrep, occ_irrep[batch], screen_rows
        )
        whole = jnp.zeros((occ_share, vir_total, FOLD), fold.dtype)
        for s in range(4):
            block = move(fold, [(r, r ^ s) for r in range(4)]) if s else fold
            whole = lax.dynamic_update_slice_in_dim(whole, block, jnp.bitwise_xor(row, s) * share, 1)
        total = dense_product(amplitudes, whole, occ_irrep, occ_local, vir_local, vir_irrep)
        quarter = (batch // 2, share, FOLD // 2)
        goals = [jnp.bitwise_xor(col, t) for t in range(4)]
        return [
            lax.dynamic_slice(total, (g // 2 * quarter[0], 0, g % 2 * quarter[2]), quarter) for g in goals
        ]

    branches = [
        sparse(0, lambda m2a, m2b, m3a, m3b: ([m2a], [])),
        sparse(0, lambda m2a, m2b, m3a, m3b: ([m2a, m2b], [])),
        sparse(0, lambda m2a, m2b, m3a, m3b: ([m2a], [m3a[:FEW_WIDE]])),
        sparse(FEW_CAPS[0], lambda m2a, m2b, m3a, m3b: ([], [m3a])),
        sparse(FEW_CAPS[1], lambda m2a, m2b, m3a, m3b: ([], [m3a, m3b])),
        sparse(0, lambda m2a, m2b, m3a, m3b: ([m2a, m2b], [m3a, m3b])),
        dense,
    ]
    quarters = lax.switch(form[0], branches, few, m2a, m2b, m3a, m3b)
    mine = quarters[0]
    for t in (1, 2, 3):
        mine = mine + lax.ppermute(quarters[t], "col", [(q, q ^ t) for q in range(4)])
    places = [(r, q) for r in range(4) for q in range(4)]
    same = lax.ppermute(mine, ("row", "col"), [(r * 4 + q, q * 4 + r) for r, q in places])
    other = lax.ppermute(mine, ("row", "col"), [(r * 4 + q, (q ^ 2) * 4 + r) for r, q in places])
    upper = row // 2 == 1
    low = jnp.where(upper, other, same)
    high = jnp.where(upper, same, other)
    return jnp.concatenate([low, high], axis=0)


def on_any(amplitudes, integrals, occ_irrep, vir_irrep, screen):
    batch, occ_share, share, vir_total = amplitudes.shape
    row = lax.axis_index("row")
    col = lax.axis_index("col")
    occ_local = lax.dynamic_slice_in_dim(occ_irrep, col * occ_share, occ_share)
    vir_local = lax.dynamic_slice_in_dim(vir_irrep, row * share, share)
    screen_rows = lax.dynamic_slice_in_dim(screen, col * occ_share, occ_share, 0)
    fold = folded_integrals(
        integrals, occ_local, vir_local, vir_irrep, occ_irrep[batch], screen_rows
    )
    whole = lax.all_gather(fold, "row", axis=1, tiled=True)
    cycle = dense_product(amplitudes, whole, occ_irrep, occ_local, vir_local, vir_irrep)
    cycle = lax.psum(cycle, "col")
    cycle = jnp.concatenate([cycle] * (vir_total // FOLD), axis=2)
    cycle = lax.all_to_all(cycle, "row", split_axis=2, concat_axis=1, tiled=True)
    a_size = vir_total // lax.axis_size("col")
    return lax.dynamic_slice_in_dim(cycle, col * a_size, a_size, 1)


def on_device(amplitudes, integrals, occ_irrep, vir_irrep, screen, occ_energy, vir_energy):
    batch, _, vir_share, vir_total = amplitudes.shape
    square = lax.axis_size("row") == 4 and lax.axis_size("col") == 4
    form = on_square if square else on_any
    cycle = form(amplitudes, integrals, occ_irrep, vir_irrep, screen)
    a_size = vir_total // lax.axis_size("col")
    return finish(
        cycle, occ_irrep, vir_irrep, occ_energy, vir_energy,
        lax.axis_index("col") * a_size, a_size, lax.axis_index("row") * vir_share, vir_share, batch,
    )


def solution(mesh):
    in_specs = (
        P("parts", "col", "row", None),
        P(("parts", "col"), "row", None),
        P("parts"),
        P("parts"),
        P("parts", None),
        P("parts"),
        P("parts"),
    )
    out_specs = P("row", "parts", "col")
    return jax.shard_map(
        on_device, mesh=mesh, in_specs=in_specs, out_specs=out_specs, check_vma=False
    )
```

profile of v0, /device:TPU:6, one launch (start us, length us, event | category | flops | bytes accessed | tf_op | source)
XLA Modules:
  0.0 114.3 jit_solution(2655011520554082316)
XLA Ops:
  0.0 0.1 pad_add_fusion.refs_3_
  0.1 6.1 %shard_map.73 = (bf16[10,3,64,128]{3,2,1,0:T(8,128)(2,1)S(1)}, bf16[22,64,256]{2,1,0:T(8,128)(2,1)S(1)}, bf16[3,64,256]{2,1,0:T(8,128)(2,1)S(1)}, bf16[22,128,25...) custom-call(s32[100]{0:T(128)} %refs_0_.1, ...), custom_call_target="tpu_custom_call" | custom-call | flops 5000000000 | bytes 15000000 | tf_op jit(solution)/shard_map/pallas_call | solution.py:179
  6.9 0.0 copy-start.5
  6.9 76.0 %conditional.1 = (f32[2,128,128]{2,1,0:T(8,128)S(1)}, f32[2,128,128]{2,1,0:T(8,128)S(1)}, f32[2,128,128]{2,1,0:T(8,128)S(1)}, f32[2,128,128]{1,0,2:T(2,128)S(1)}) conditional(s32[]{:T(128)} %bitcast.21, (s32[512]{0:T(512)S(1)}, s32[100]{0:T(128)S(1)}, s32[2]{0:T(128)S(1)}, s32[25]{0:T(128)S(1)}, ...), branch_computations={%region_0.0_spmd, %region_1.0_spmd, %region_2.0_spmd, %region_3.0_... | conditional | flops 25001842688 | bytes 130558976 | solution.py:654
  6.9 3.5 %collective-permute-start.20 = (bf16[22,64,256]{2,1,0:T(8,128)(2,1)S(1)}, bf16[22,64,256]{2,1,0:T(8,128)(2,1)S(1)}, u32[]{:S(2)}, u32[]{:S(2)}) collective-permute-start(bf16[22,64,256]{2,1,0:T(8,128)(2,1)S(1)} %get-tuple-element.180), channel_id=1, source_target_pairs={{0,4},{12,8},{1,5},{13,9},{2,6},{14,10},{3,7},{15,11},{16,20},{28,... | collective-permute-start | bytes 2162696 | tf_op jit(solution)/shard_map/cond/branch_0_fun/ppermute | solution.py:586
  10.5 4.9 %branch_0_fun.5.refs_0_ = bf16[25,64,128]{2,1,0:T(8,128)(2,1)S(1)} custom-call(s32[100]{0:T(128)S(1)} %get-tuple-element.167.refs_0_.occ_ref, s32[512]{0:T(512)S(1)} %get-tuple-element.168.refs_1_.vir_ref, s32[8,100]{1,0:T(8,128)S(1)} %bitcast.74, s32[2]{0:T(128)S(1)} %get-tuple-element.172.refs_1_.refs_3_.place_ref, ...), custom_call_target="tpu_custom_call" | custom-call | flops 5000000000 | bytes 15000000 | tf_op jit(solution)/shard_map/cond/branch_0_fun/pallas_call | solution.py:237
  15.4 0.7 collective-permute-start.21
  16.1 1.3 %collective-permute-start.22 = (bf16[25,64,128]{2,1,0:T(8,128)(2,1)S(1)}, bf16[25,64,128]{2,1,0:T(8,128)(2,1)S(1)}, u32[]{:S(2)}, u32[]{:S(2)}) collective-permute-start(bf16[25,64,128]{2,1,0:T(8,128)(2,1)S(1)} %branch_0_fun.5.refs_0_), channel_id=1, source_target_pairs={{4,0},{8,12},{5,1},{9,13},{6,2},{10,14},{7,3},{11,15},{20,16},{24,... | collective-permute-start | bytes 1228808 | tf_op jit(solution)/shard_map/cond/branch_0_fun/ppermute | solution.py:586
  17.4 9.0 %branch_0_fun.4 = (bf16[5,512,1920]{2,1,0:T(8,128)(2,1)S(1)}, bf16[5,512,640]{2,1,0:T(8,128)(2,1)S(1)}, bf16[5,512,640]{2,1,0:T(8,128)(2,1)S(1)}) custom-call(s32[100]{0:T(128)S(1)} %get-tuple-element.167.refs_0_.occ_ref, s32[2]{0:T(128)S(1)} %get-tuple-element.172.refs_1_.refs_3_.place_ref, s32[25]{0:T(128)S(1)} %get-tuple-element.173.refs_2_.posx_ref, ...), custom_call_target="tpu_custom_call" | custom-call | flops 7000000000 | bytes 21000000 | tf_op jit(solution)/shard_map/cond/branch_0_fun/pallas_call | solution.py:362
  26.4 2.6 %collective-permute-done.22 = bf16[25,64,128]{2,1,0:T(8,128)(2,1)S(1)} collective-permute-done((bf16[25,64,128]{2,1,0:T(8,128)(2,1)S(1)}, bf16[25,64,128]{2,1,0:T(8,128)(2,1)S(1)}, u32[]{:S(2)}, u32[]{:S(2)}) %collective-permute-start.22) | collective-permute-done | bytes 409632 | tf_op jit(solution)/shard_map/cond/branch_0_fun/ppermute | solution.py:586
  29.0 0.2 add.123
  29.2 0.7 collective-permute-start.23
  30.0 4.9 %collective-permute-start.24 = (bf16[25,64,128]{2,1,0:T(8,128)(2,1)S(1)}, bf16[25,64,128]{2,1,0:T(8,128)(2,1)S(1)}, u32[]{:S(2)}, u32[]{:S(2)}) collective-permute-start(bf16[25,64,128]{2,1,0:T(8,128)(2,1)S(1)} %branch_0_fun.5.refs_0_), channel_id=1, source_target_pairs={{0,4},{12,8},{1,5},{13,9},{2,6},{14,10},{3,7},{15,11},{16,20},{28,... | collective-permute-start | bytes 1228808 | tf_op jit(solution)/shard_map/cond/branch_0_fun/ppermute | solution.py:586
  34.9 1.3 %collective-permute-start.25 = (bf16[25,64,128]{2,1,0:T(8,128)(2,1)S(1)}, bf16[25,64,128]{2,1,0:T(8,128)(2,1)S(1)}, u32[]{:S(2)}, u32[]{:S(2)}) collective-permute-start(bf16[25,64,128]{2,1,0:T(8,128)(2,1)S(1)} %collective-permute-done.21.refs_2_), channel_id=1, source_target_pairs={{4,0},{8,12},{5,1},{9,13},{6,2},{10,14},{7,3},{11,15},{20,16},{24,... | collective-permute-start | bytes 1228808 | tf_op jit(solution)/shard_map/cond/branch_0_fun/ppermute | solution.py:586
  36.2 6.6 %collective-permute-done.24 = bf16[25,64,128]{2,1,0:T(8,128)(2,1)S(1)} collective-permute-done((bf16[25,64,128]{2,1,0:T(8,128)(2,1)S(1)}, bf16[25,64,128]{2,1,0:T(8,128)(2,1)S(1)}, u32[]{:S(2)}, u32[]{:S(2)}) %collective-permute-start.24) | collective-permute-done | bytes 409632 | tf_op jit(solution)/shard_map/cond/branch_0_fun/ppermute | solution.py:586
  42.8 0.1 add.124.refs_1_
  42.9 4.0 %collective-permute-done.25.refs_3_ = bf16[25,64,128]{2,1,0:T(8,128)(2,1)S(1)} collective-permute-done((bf16[25,64,128]{2,1,0:T(8,128)(2,1)S(1)}, bf16[25,64,128]{2,1,0:T(8,128)(2,1)S(1)}, u32[]{:S(2)}, u32[]{:S(2)}) %collective-permute-start.25) | collective-permute-done | bytes 409632 | tf_op jit(solution)/shard_map/cond/branch_0_fun/ppermute | solution.py:586
  46.9 0.2 add.126
  47.2 1.3 %collective-permute-start.28 = (bf16[22,64,256]{2,1,0:T(8,128)(2,1)S(1)}, bf16[22,64,256]{2,1,0:T(8,128)(2,1)S(1)}, u32[]{:S(2)}, u32[]{:S(2)}) collective-permute-start(bf16[22,64,256]{2,1,0:T(8,128)(2,1)S(1)} %add.126), channel_id=1, source_target_pairs={{4,0},{8,12},{5,1},{9,13},{6,2},{10,14},{7,3},{11,15},{20,16},{24,... | collective-permute-start | bytes 2162696 | tf_op jit(solution)/shard_map/cond/branch_0_fun/ppermute | solution.py:586
  48.5 0.7 collective-permute-start.26
  49.2 1.3 %collective-permute-start.27 = (bf16[25,64,128]{2,1,0:T(8,128)(2,1)S(1)}, bf16[25,64,128]{2,1,0:T(8,128)(2,1)S(1)}, u32[]{:S(2)}, u32[]{:S(2)}) collective-permute-start(bf16[25,64,128]{2,1,0:T(8,128)(2,1)S(1)} %collective-permute-done.26.refs_4_), channel_id=1, source_target_pairs={{4,0},{8,12},{5,1},{9,13},{6,2},{10,14},{7,3},{11,15},{20,16},{24,... | collective-permute-start | bytes 1228808 | tf_op jit(solution)/shard_map/cond/branch_0_fun/ppermute | solution.py:586
  50.5 17.7 %collective-permute-done.28 = bf16[22,64,256]{2,1,0:T(8,128)(2,1)S(1)} collective-permute-done((bf16[22,64,256]{2,1,0:T(8,128)(2,1)S(1)}, bf16[22,64,256]{2,1,0:T(8,128)(2,1)S(1)}, u32[]{:S(2)}, u32[]{:S(2)}) %collective-permute-start.28) | collective-permute-done | bytes 720928 | tf_op jit(solution)/shard_map/cond/branch_0_fun/ppermute | solution.py:586
  68.2 0.1 add_add_fusion.refs_0_
  68.3 5.5 %collective-permute-done.27.refs_5_ = bf16[25,64,128]{2,1,0:T(8,128)(2,1)S(1)} collective-permute-done((bf16[25,64,128]{2,1,0:T(8,128)(2,1)S(1)}, bf16[25,64,128]{2,1,0:T(8,128)(2,1)S(1)}, u32[]{:S(2)}, u32[]{:S(2)}) %collective-permute-start.27) | collective-permute-done | bytes 409632 | tf_op jit(solution)/shard_map/cond/branch_0_fun/ppermute | solution.py:586
  73.8 5.6 %branch_0_fun.6 = (f32[512,128]{1,0:T(8,128)S(1)}, f32[16,256]{1,0:T(8,128)S(1)}) custom-call(s32[25]{0:T(128)S(1)} %get-tuple-element.170.pos3_ref, s32[25]{0:T(128)S(1)} %get-tuple-element.173.refs_2_.posx_ref, s32[2]{0:T(128)S(1)} %get-tuple-element.172.refs_1_.refs_3_.place_ref, bf16[5,512,1920]{2,1,0:T(8,128)(2,1)S(1)} %get-tuple-element.176.lhs_ref, ...), custom_call_target="tpu_custom_call" | custom-call | flops 6000000000 | bytes 18000000 | tf_op jit(solution)/shard_map/cond/branch_0_fun/pallas_call | solution.py:432
  79.4 2.8 %branch_0_fun.7 = (f32[2,128,128]{2,1,0:T(8,128)S(1)}, f32[2,128,128]{2,1,0:T(8,128)S(1)}, f32[2,128,128]{2,1,0:T(8,128)S(1)}, f32[2,128,128]{2,1,0:T(8,128)S(1)}) custom-call(s32[100]{0:T(128)S(1)} %get-tuple-element.167.refs_0_.occ_ref, s32[512]{0:T(512)S(1)} %get-tuple-element.168.refs_1_.vir_ref, s32[25]{0:T(128)S(1)} %get-tuple-element.169.pos2_ref, ...), custom_call_target="tpu_custom_call" | custom-call | flops 2000000000 | bytes 6000000 | tf_op jit(solution)/shard_map/cond/branch_0_fun/pallas_call | solution.py:523
  82.2 0.1 copy.19
  82.9 0.1 copy.17
  83.0 13.1 %collective-permute-start.79 = (f32[2,128,128]{1,0,2:T(2,128)S(1)}, f32[2,128,128]{1,0,2:T(2,128)S(1)}, u32[]{:S(2)}, u32[]{:S(2)}) collective-permute-start(f32[2,128,128]{1,0,2:T(2,128)S(1)} %copy.17), channel_id=1, source_target_pairs={{0,3},{1,2},{2,1},{3,0},{4,7},{5,6},{6,5},{7,4},{8,11},{9,10},{10,... | collective-permute-start | bytes 393224 | tf_op jit(solution)/shard_map/ppermute | solution.py:657
  96.1 0.1 copy.16
  96.2 0.1 collective-permute-start.78
  96.3 0.1 copy.14
  96.4 0.2 collective-permute-start.77
  96.6 0.6 slice.31
  97.1 0.6 slice.33
  97.7 0.6 slice_add_fusion.1
  98.4 0.1 fusion.13
  98.5 0.1 broadcast_subtract_fusion
  98.5 0.6 slice_xor_fusion
  99.2 0.1 fusion.12
  99.3 0.3 collective-permute-done.79
  99.6 1.9 %collective-permute-done.78 = f32[2,128,128]{1,0,2:T(2,128)S(1)} collective-permute-done((f32[2,128,128]{1,0,2:T(2,128)S(1)}, f32[2,128,128]{1,0,2:T(2,128)S(1)}, u32[]{:S(2)}, u32[]{:S(2)}) %collective-permute-start.78) | collective-permute-done | bytes 131104 | tf_op jit(solution)/shard_map/ppermute | solution.py:657
  101.6 2.0 %collective-permute-start.80 = (f32[2,128,128]{1,0,2:T(2,128)S(1)}, f32[2,128,128]{1,0,2:T(2,128)S(1)}, u32[]{:S(2)}, u32[]{:S(2)}) collective-permute-start(f32[2,128,128]{1,0,2:T(2,128)S(1)} %bitcast.50), channel_id=1, source_target_pairs={{0,8},{1,12},{2,0},{3,4},{4,9},{5,13},{6,1},{7,5},{8,10},{9,14},{1... | collective-permute-start | bytes 393224 | tf_op jit(solution)/shard_map/ppermute | solution.py:660
  103.6 1.9 %collective-permute-start.81 = (f32[2,128,128]{1,0,2:T(2,128)S(1)}, f32[2,128,128]{1,0,2:T(2,128)S(1)}, u32[]{:S(2)}, u32[]{:S(2)}) collective-permute-start(f32[2,128,128]{1,0,2:T(2,128)S(1)} %bitcast.51), channel_id=1, source_target_pairs={{0,0},{1,4},{2,8},{3,12},{4,1},{5,5},{6,9},{7,13},{8,2},{9,6},{10,... | collective-permute-start | bytes 393224 | tf_op jit(solution)/shard_map/ppermute | solution.py:659
  105.5 0.1 broadcast_xor_fusion.2
  105.5 3.5 %collective-permute-done.80 = f32[2,128,128]{1,0,2:T(2,128)S(1)} collective-permute-done((f32[2,128,128]{1,0,2:T(2,128)S(1)}, f32[2,128,128]{1,0,2:T(2,128)S(1)}, u32[]{:S(2)}, u32[]{:S(2)}) %collective-permute-start.80) | collective-permute-done | bytes 131104 | tf_op jit(solution)/shard_map/ppermute | solution.py:660
  109.1 4.2 %collective-permute-done.81 = f32[2,128,128]{1,0,2:T(2,128)S(1)} collective-permute-done((f32[2,128,128]{1,0,2:T(2,128)S(1)}, f32[2,128,128]{1,0,2:T(2,128)S(1)}, u32[]{:S(2)}, u32[]{:S(2)}) %collective-permute-start.81) | collective-permute-done | bytes 131104 | tf_op jit(solution)/shard_map/ppermute | solution.py:659
  113.3 1.0 fusion.11
  (17 shorter events, 0.1 us)
Async XLA Ops:
  0.1 6.8 %copy-start.1 = (s32[512]{0:T(512)S(1)}, s32[512]{0:T(512)}, u32[]{:S(2)}) copy-start(s32[512]{0:T(512)} %refs_1_.1) | copy-start | bytes 6148
  0.1 6.8 %copy-start.2 = (s32[100,8]{0,1:T(8,128)S(1)}, s32[100,8]{0,1:T(8,128)}, u32[]{:S(2)}) copy-start(s32[100,8]{0,1:T(8,128)} %param.18) | copy-start | bytes 9604
  0.1 6.8 %copy-start.3 = (s32[100]{0:T(128)S(1)}, s32[100]{0:T(128)}, u32[]{:S(2)}) copy-start(s32[100]{0:T(128)} %refs_0_.1) | copy-start | bytes 1204
  6.9 90.3 %copy-start.5 = (f32[100]{0:T(128)S(1)}, f32[100]{0:T(128)}, u32[]{:S(2)}) copy-start(f32[100]{0:T(128)} %param.19) | copy-start | bytes 1204
  6.9 91.5 %copy-start.4 = (f32[512]{0:T(512)S(1)}, f32[512]{0:T(512)}, u32[]{:S(2)}) copy-start(f32[512]{0:T(512)} %param.20) | copy-start | bytes 6148
  6.9 22.1 %collective-permute-start.20 = (bf16[22,64,256]{2,1,0:T(8,128)(2,1)S(1)}, bf16[22,64,256]{2,1,0:T(8,128)(2,1)S(1)}, u32[]{:S(2)}, u32[]{:S(2)}) collective-permute-start(bf16[22,64,256]{2,1,0:T(8,128)(2,1)S(1)} %get-tuple-element.180), channel_id=1, source_target_pairs={{0,4},{12,8},{1,5},{13,9},{2,6},{14,10},{3,7},{15,11},{16,20},{28,... | collective-permute-start | bytes 2162696 | tf_op jit(solution)/shard_map/cond/branch_0_fun/ppermute | solution.py:586
  15.4 11.0 %collective-permute-start.21 = (bf16[25,64,128]{2,1,0:T(8,128)(2,1)S(1)}, bf16[25,64,128]{2,1,0:T(8,128)(2,1)S(1)}, u32[]{:S(2)}, u32[]{:S(2)}) collective-permute-start(bf16[25,64,128]{2,1,0:T(8,128)(2,1)S(1)} %branch_0_fun.5.refs_0_), channel_id=1, source_target_pairs={{4,8},{8,4},{5,9},{9,5},{6,10},{10,6},{7,11},{11,7},{20,24},{24,20... | collective-permute-start | bytes 1228808 | tf_op jit(solution)/shard_map/cond/branch_0_fun/ppermute | solution.py:586
  16.1 12.9 %collective-permute-start.22 = (bf16[25,64,128]{2,1,0:T(8,128)(2,1)S(1)}, bf16[25,64,128]{2,1,0:T(8,128)(2,1)S(1)}, u32[]{:S(2)}, u32[]{:S(2)}) collective-permute-start(bf16[25,64,128]{2,1,0:T(8,128)(2,1)S(1)} %branch_0_fun.5.refs_0_), channel_id=1, source_target_pairs={{4,0},{8,12},{5,1},{9,13},{6,2},{10,14},{7,3},{11,15},{20,16},{24,... | collective-permute-start | bytes 1228808 | tf_op jit(solution)/shard_map/cond/branch_0_fun/ppermute | solution.py:586
  29.2 17.7 %collective-permute-start.23 = (bf16[22,64,256]{2,1,0:T(8,128)(2,1)S(1)}, bf16[22,64,256]{2,1,0:T(8,128)(2,1)S(1)}, u32[]{:S(2)}, u32[]{:S(2)}) collective-permute-start(bf16[22,64,256]{2,1,0:T(8,128)(2,1)S(1)} %add.123), channel_id=1, source_target_pairs={{4,8},{8,4},{5,9},{9,5},{6,10},{10,6},{7,11},{11,7},{20,24},{24,20... | collective-permute-start | bytes 2162696 | tf_op jit(solution)/shard_map/cond/branch_0_fun/ppermute | solution.py:586
  30.0 12.8 %collective-permute-start.24 = (bf16[25,64,128]{2,1,0:T(8,128)(2,1)S(1)}, bf16[25,64,128]{2,1,0:T(8,128)(2,1)S(1)}, u32[]{:S(2)}, u32[]{:S(2)}) collective-permute-start(bf16[25,64,128]{2,1,0:T(8,128)(2,1)S(1)} %branch_0_fun.5.refs_0_), channel_id=1, source_target_pairs={{0,4},{12,8},{1,5},{13,9},{2,6},{14,10},{3,7},{15,11},{16,20},{28,... | collective-permute-start | bytes 1228808 | tf_op jit(solution)/shard_map/cond/branch_0_fun/ppermute | solution.py:586
  34.9 12.1 %collective-permute-start.25 = (bf16[25,64,128]{2,1,0:T(8,128)(2,1)S(1)}, bf16[25,64,128]{2,1,0:T(8,128)(2,1)S(1)}, u32[]{:S(2)}, u32[]{:S(2)}) collective-permute-start(bf16[25,64,128]{2,1,0:T(8,128)(2,1)S(1)} %collective-permute-done.21.refs_2_), channel_id=1, source_target_pairs={{4,0},{8,12},{5,1},{9,13},{6,2},{10,14},{7,3},{11,15},{20,16},{24,... | collective-permute-start | bytes 1228808 | tf_op jit(solution)/shard_map/cond/branch_0_fun/ppermute | solution.py:586
  47.2 21.0 %collective-permute-start.28 = (bf16[22,64,256]{2,1,0:T(8,128)(2,1)S(1)}, bf16[22,64,256]{2,1,0:T(8,128)(2,1)S(1)}, u32[]{:S(2)}, u32[]{:S(2)}) collective-permute-start(bf16[22,64,256]{2,1,0:T(8,128)(2,1)S(1)} %add.126), channel_id=1, source_target_pairs={{4,0},{8,12},{5,1},{9,13},{6,2},{10,14},{7,3},{11,15},{20,16},{24,... | collective-permute-start | bytes 2162696 | tf_op jit(solution)/shard_map/cond/branch_0_fun/ppermute | solution.py:586
  48.5 0.7 collective-permute-start.26
  49.2 24.6 %collective-permute-start.27 = (bf16[25,64,128]{2,1,0:T(8,128)(2,1)S(1)}, bf16[25,64,128]{2,1,0:T(8,128)(2,1)S(1)}, u32[]{:S(2)}, u32[]{:S(2)}) collective-permute-start(bf16[25,64,128]{2,1,0:T(8,128)(2,1)S(1)} %collective-permute-done.26.refs_4_), channel_id=1, source_target_pairs={{4,0},{8,12},{5,1},{9,13},{6,2},{10,14},{7,3},{11,15},{20,16},{24,... | collective-permute-start | bytes 1228808 | tf_op jit(solution)/shard_map/cond/branch_0_fun/ppermute | solution.py:586
  83.0 16.6 %collective-permute-start.79 = (f32[2,128,128]{1,0,2:T(2,128)S(1)}, f32[2,128,128]{1,0,2:T(2,128)S(1)}, u32[]{:S(2)}, u32[]{:S(2)}) collective-permute-start(f32[2,128,128]{1,0,2:T(2,128)S(1)} %copy.17), channel_id=1, source_target_pairs={{0,3},{1,2},{2,1},{3,0},{4,7},{5,6},{6,5},{7,4},{8,11},{9,10},{10,... | collective-permute-start | bytes 393224 | tf_op jit(solution)/shard_map/ppermute | solution.py:657
  96.2 5.3 %collective-permute-start.78 = (f32[2,128,128]{1,0,2:T(2,128)S(1)}, f32[2,128,128]{1,0,2:T(2,128)S(1)}, u32[]{:S(2)}, u32[]{:S(2)}) collective-permute-start(f32[2,128,128]{1,0,2:T(2,128)S(1)} %copy.16), channel_id=1, source_target_pairs={{0,2},{1,3},{2,0},{3,1},{4,6},{5,7},{6,4},{7,5},{8,10},{9,11},{10,... | collective-permute-start | bytes 393224 | tf_op jit(solution)/shard_map/ppermute | solution.py:657
  96.4 5.2 %collective-permute-start.77 = (f32[2,128,128]{1,0,2:T(2,128)S(1)}, f32[2,128,128]{1,0,2:T(2,128)S(1)}, u32[]{:S(2)}, u32[]{:S(2)}) collective-permute-start(f32[2,128,128]{1,0,2:T(2,128)S(1)} %copy.14), channel_id=1, source_target_pairs={{0,1},{1,0},{2,3},{3,2},{4,5},{5,4},{6,7},{7,6},{8,9},{9,8},{10,11... | collective-permute-start | bytes 393224 | tf_op jit(solution)/shard_map/ppermute | solution.py:657
  101.6 7.5 %collective-permute-start.80 = (f32[2,128,128]{1,0,2:T(2,128)S(1)}, f32[2,128,128]{1,0,2:T(2,128)S(1)}, u32[]{:S(2)}, u32[]{:S(2)}) collective-permute-start(f32[2,128,128]{1,0,2:T(2,128)S(1)} %bitcast.50), channel_id=1, source_target_pairs={{0,8},{1,12},{2,0},{3,4},{4,9},{5,13},{6,1},{7,5},{8,10},{9,14},{1... | collective-permute-start | bytes 393224 | tf_op jit(solution)/shard_map/ppermute | solution.py:660
  103.6 9.7 %collective-permute-start.81 = (f32[2,128,128]{1,0,2:T(2,128)S(1)}, f32[2,128,128]{1,0,2:T(2,128)S(1)}, u32[]{:S(2)}, u32[]{:S(2)}) collective-permute-start(f32[2,128,128]{1,0,2:T(2,128)S(1)} %bitcast.51), channel_id=1, source_target_pairs={{0,0},{1,4},{2,8},{3,12},{4,1},{5,5},{6,9},{7,13},{8,2},{9,6},{10,... | collective-permute-start | bytes 393224 | tf_op jit(solution)/shard_map/ppermute | solution.py:659
where the time goes:
time: 113 us; the launch traced here: 114 us
  waiting for transfers between devices  46.4 us (41%)
  starting transfers between devices  32.9 us (29%)
  Pallas kernels  28.5 us (25%)
  other arithmetic  3.29 us (3%)
  local copies, waits for them, and re-layouts  1.81 us (2%)
    ppermute x9, waiting for transfers between devices, move(): return lax.ppermute(v, 'row', pairs)  36.4 us
    ppermute x9, starting transfers between devices, move(): return lax.ppermute(v, 'row', pairs)  15.7 us
    ppermute x3, starting transfers between devices, on_square(): lax.ppermute(quarters[t], 'col', [(q, q ^ t) for q in range(4)])  13.3 us
    pallas_call x1, Pallas kernels, masked_amplitudes(): pl.pallas_call(kernel, in_specs=[smem, smem, smem, hbm, vmem], out_specs=...  9 us
    pallas_call x1, Pallas kernels, wide_blocks(): pl.pallas_call(kernel, grid_spec=pltpu.PrefetchScalarGridSpec(num_scalar_...  6.15 us
    pallas_call x1, Pallas kernels, first_product(): pl.pallas_call(make_first_kernel(few, len(m3), starts_of([v[0] for v in m...  5.61 us
    pallas_call x1, Pallas kernels, narrow_blocks(): pl.pallas_call(kernel, grid_spec=pltpu.PrefetchScalarGridSpec(num_scalar_...  4.94 us
    ppermute x1, waiting for transfers between devices, on_square(): lax.ppermute(mine, ('row', 'col'), [(r * 4 + q, q * 4 + r) for r, q in pl...  4.18 us
  transfers between devices with their start and end apart: 14, of which 9 were waited for; matrix products, arithmetic and copies ran while one was open for 3% of the time, Pallas kernels for 12%

commit v1 on v0

--- a/solution.py
+++ b/solution.py
@@ -75,36 +75,49 @@
     return bits
 
 
+def copy_of(source_ref, int_ref, sems, group):
+    here = pl.ds(group * K_STEP, K_STEP)
+    return pltpu.make_async_copy(source_ref.at[here], int_ref.at[here], sems.at[group])
+
+
+def start_copies(source_ref, int_ref, sems):
+    for group in range(int_ref.shape[0] // K_STEP):
+        copy_of(source_ref, int_ref, sems, group).start()
+
+
+def wait_copy(source_ref, int_ref, sems, group):
+    copy_of(source_ref, int_ref, sems, group).wait()
+
+
 def wide_kernel(
-    occ_ref, vir_ref, screen_ref, place_ref, int_ref, row_ref,
+    occ_ref, vir_ref, screen_ref, place_ref, source_ref, row_ref,
     few_ref, m2a_ref, m2b_ref, m3a_ref, m3b_ref, pos2_ref, pos3_ref, posx_ref, form_ref, count_ref,
-    mix_ref, small_mix_ref, column_ref, counts_ref, batch,
+    mix_ref, small_mix_ref, column_ref, counts_ref, int_ref, sems, batch,
 ):
-    step = pl.program_id(0)
-    k_step, depth, total = int_ref.shape
+    start_copies(source_ref, int_ref, sems)
+    k_all, depth, total = int_ref.shape
     half = depth // 2
     row, col = place_ref[0], place_ref[1]
     pair_label = occ_ref[batch]
     big = largest_irrep(vir_ref)
-    k_all = k_step * pl.num_programs(0)
     mostly_zero = (occ_ref[col * k_all] == pair_label) | (occ_ref[(col + 1) * k_all - 1] == pair_label)
     most = FEW_CAPS[-1]
-
-    @pl.when(step == 0)
+    for n in range(3):
+        counts_ref[n] = 0
+    label_mix(mix_ref, column_ref, row_ref, row, big, True)
+
+    @pl.when(mostly_zero)
     def _():
-        for n in range(3):
-            counts_ref[n] = 0
-        label_mix(mix_ref, column_ref, row_ref, row, big, True)
-
-        @pl.when(mostly_zero)
+        label_mix(small_mix_ref, column_ref, row_ref, row, big, False)
+
+    local = column_ref[pl.ds(pl.multiple_of(row * depth, depth), depth), :1]
+
+    @pl.loop(0, k_all)
+    def _(k):
+        @pl.when(k % K_STEP == 0)
         def _():
-            label_mix(small_mix_ref, column_ref, row_ref, row, big, False)
-
-    local = column_ref[pl.ds(pl.multiple_of(row * depth, depth), depth), :1]
-
-    @pl.loop(0, k_step)
-    def _(j):
-        k = step * k_step + j
+            wait_copy(source_ref, int_ref, sems, k // K_STEP)
+
         k_whole = col * k_all + k
         x = jnp.bitwise_xor(occ_ref[k_whole], pair_label)
         on_big = screen_ref[jnp.bitwise_xor(big, x), k_whole] == 1
@@ -116,13 +129,13 @@
 
         @pl.when(pos2 >= 0)
         def _():
-            wide = kept_folded(int_ref, mix_ref, j, x)
+            wide = kept_folded(int_ref, mix_ref, k, x)
             short = wide[:half] + wide[half:]
 
-            @pl.when(mostly_zero & (pos2 < most))
+            @pl.when(mostly_zero & (posx < most))
             def _():
                 for piece in range(2):
-                    few_ref[pos2, 1 + piece] = short[:, piece * 2 * NARROW:(piece + 1) * 2 * NARROW]
+                    few_ref[posx, 1 + piece] = short[:, piece * 2 * NARROW:(piece + 1) * 2 * NARROW]
 
             @pl.when(pos2 < CAPS[0])
             def _():
@@ -134,12 +147,17 @@
 
         @pl.when(mostly_zero & (posx >= 0) & (posx < most))
         def _():
-            kept = kept_folded(int_ref, small_mix_ref, j, x)
+            kept = kept_folded(int_ref, small_mix_ref, k, x)
             few_ref[posx, 0] = narrow_fold(kept, screen_bits(screen_ref, k_whole), local)
+
+            @pl.when(pos2 < 0)
+            def _():
+                for piece in range(2):
+                    few_ref[posx, 1 + piece] = jnp.zeros((half, 2 * NARROW), jnp.bfloat16)
 
         @pl.when(pos3 >= 0)
         def _():
-            wide = kept_folded(int_ref, mix_ref, j, x)
+            wide = kept_folded(int_ref, mix_ref, k, x)
 
             @pl.when(pos3 < CAPS[0])
             def _():
@@ -149,22 +167,20 @@
             def _():
                 m3b_ref[pos3 - CAPS[0]] = wide
 
-    @pl.when(step == pl.num_programs(0) - 1)
-    def _():
-        labels = row_ref[...]
-        lanes = lax.broadcasted_iota(jnp.int32, labels.shape, 1)
-        ahead = pltpu.roll(labels, total - NARROW, 1)
-        long = (labels == ahead) & (lanes < total - NARROW) & (labels != big)
-        too_long = jnp.max(long.astype(jnp.int32)) == 1
-        n2, n3, nx = counts_ref[0], counts_ref[1], counts_ref[2]
-        count_ref[0] = nx
-        one_label = occ_ref[0] == pair_label
-        form = jnp.where((nx <= FEW_CAPS[0]) & (n3 <= CAPS[0]), 3, jnp.where(nx <= FEW_CAPS[1], 4, 5))
-        form = jnp.where(mostly_zero, form, 5)
-        form = jnp.where((n3 <= FEW_WIDE) & (n2 <= CAPS[0]), 2, form)
-        form = jnp.where(one_label, form, 6)
-        form = jnp.where(n3 == 0, jnp.where(n2 <= CAPS[0], 0, 1), form)
-        form_ref[0] = jnp.where(too_long, 6, form)
+    labels = row_ref[...]
+    lanes = lax.broadcasted_iota(jnp.int32, labels.shape, 1)
+    ahead = pltpu.roll(labels, total - NARROW, 1)
+    long = (labels == ahead) & (lanes < total - NARROW) & (labels != big)
+    too_long = jnp.max(long.astype(jnp.int32)) == 1
+    n2, n3, nx = counts_ref[0], counts_ref[1], counts_ref[2]
+    count_ref[0] = nx
+    one_label = occ_ref[0] == pair_label
+    form = jnp.where((nx <= FEW_CAPS[0]) & (n3 <= CAPS[0]), 3, jnp.where(nx <= FEW_CAPS[1], 4, 5))
+    form = jnp.where(mostly_zero, form, 5)
+    form = jnp.where((n3 <= FEW_WIDE) & (n2 <= CAPS[0]), 2, form)
+    form = jnp.where(one_label, form, 6)
+    form = jnp.where(n3 == 0, jnp.where(n2 <= CAPS[0], 0, 1), form)
+    form_ref[0] = jnp.where(too_long, 6, form)
 
 
 def wide_blocks(integrals, occ_irrep, vir_irrep, screen, place, batch):
@@ -176,25 +192,19 @@
     def kernel(*refs):
         wide_kernel(*refs, batch)
 
+    vmem = pl.BlockSpec(memory_space=pltpu.VMEM)
     return pl.pallas_call(
         kernel,
-        grid_spec=pltpu.PrefetchScalarGridSpec(
-            num_scalar_prefetch=4,
-            grid=(occ_share // K_STEP,),
-            in_specs=[
-                pl.BlockSpec((K_STEP, depth, total), lambda k, *_: (k, 0, 0)),
-                pl.BlockSpec((1, total), lambda k, *_: (0, 0)),
-            ],
-            out_specs=[pl.BlockSpec(few, lambda k, *_: (0, 0, 0, 0))]
-            + [pl.BlockSpec(v, lambda k, *_: (0, 0, 0)) for v in shapes]
-            + [smem] * 5,
-            scratch_shapes=[
-                pltpu.VMEM((depth, total), jnp.bfloat16),
-                pltpu.VMEM((depth, total), jnp.bfloat16),
-                pltpu.VMEM((total, 8), jnp.int32),
-                pltpu.SMEM((3,), jnp.int32),
-            ],
-        ),
+        in_specs=[smem] * 4 + [pl.BlockSpec(memory_space=pltpu.HBM), vmem],
+        out_specs=[vmem] * (1 + len(shapes)) + [smem] * 5,
+        scratch_shapes=[
+            pltpu.VMEM((depth, total), jnp.bfloat16),
+            pltpu.VMEM((depth, total), jnp.bfloat16),
+            pltpu.VMEM((total, 8), jnp.int32),
+            pltpu.SMEM((3,), jnp.int32),
+            pltpu.VMEM(integrals.shape, jnp.bfloat16),
+            pltpu.SemaphoreType.DMA((occ_share // K_STEP,)),
+        ],
         out_shape=[jax.ShapeDtypeStruct(v, jnp.bfloat16) for v in [few] + shapes]
         + [jax.ShapeDtypeStruct((n,), jnp.int32) for n in (occ_share, occ_share, occ_share, 1, 1)],
         cost_estimate=cost(5),
@@ -203,51 +213,52 @@
 
 
 def narrow_kernel(
-    occ_ref, vir_ref, screen_ref, place_ref, int_ref, row_ref, few_ref, narrow_ref, mix_ref, column_ref, batch,
+    occ_ref, vir_ref, screen_ref, place_ref, source_ref, row_ref, few_ref, narrow_ref,
+    mix_ref, column_ref, int_ref, sems, batch,
 ):
-    step = pl.program_id(0)
-    k_step, depth, total = int_ref.shape
+    start_copies(source_ref, int_ref, sems)
+    k_all, depth, total = int_ref.shape
     row, col = place_ref[0], place_ref[1]
-
-    @pl.when(step == 0)
-    def _():
-        label_mix(mix_ref, column_ref, row_ref, row, largest_irrep(vir_ref), False)
-        if few_ref is not None:
-            for n in range(few_ref.shape[0]):
-                for piece in range(2):
-                    narrow_ref[k_step * pl.num_programs(0) + 2 * n + piece] = few_ref[n, 1 + piece]
-
+    label_mix(mix_ref, column_ref, row_ref, row, largest_irrep(vir_ref), False)
+    if few_ref is not None:
+        for n in range(few_ref.shape[0]):
+            for piece in range(2):
+                narrow_ref[k_all + 2 * n + piece] = few_ref[n, 1 + piece]
     local = column_ref[pl.ds(pl.multiple_of(row * depth, depth), depth), :1]
-    for j in range(k_step):
-        k_whole = (col * pl.num_programs(0) + step) * k_step + j
-        x = jnp.bitwise_xor(occ_ref[k_whole], occ_ref[batch])
-        kept = kept_folded(int_ref, mix_ref, j, x)
-        narrow_ref[step * k_step + j] = narrow_fold(kept, screen_bits(screen_ref, k_whole), local)
+
+    @pl.loop(0, k_all // K_STEP)
+    def _(group):
+        wait_copy(source_ref, int_ref, sems, group)
+        for j in range(K_STEP):
+            k = group * K_STEP + j
+            k_whole = col * k_all + k
+            x = jnp.bitwise_xor(occ_ref[k_whole], occ_ref[batch])
+            kept = kept_folded(int_ref, mix_ref, k, x)
+            narrow_ref[k] = narrow_fold(kept, screen_bits(screen_ref, k_whole), local)
 
 
 def narrow_blocks(integrals, occ_irrep, vir_irrep, screen, place, few, batch):
     occ_share, depth, total = integrals.shape
     extra = [] if few is None else [few]
     count = occ_share + sum(2 * v.shape[0] for v in extra)
-    shape = (count, depth // 2, 2 * NARROW)
+    smem = pl.BlockSpec(memory_space=pltpu.SMEM)
+    vmem = pl.BlockSpec(memory_space=pltpu.VMEM)
 
     def kernel(*refs):
         narrow_kernel(*(refs if extra else refs[:6] + (None,) + refs[6:]), batch)
 
     return pl.pallas_call(
         kernel,
-        grid_spec=pltpu.PrefetchScalarGridSpec(
-            num_scalar_prefetch=4,
-            grid=(occ_share // K_STEP,),
-            in_specs=[
-                pl.BlockSpec((K_STEP, depth, total), lambda k, *_: (k, 0, 0)),
-                pl.BlockSpec((1, total), lambda k, *_: (0, 0)),
-            ] + [pl.BlockSpec(v.shape, lambda k, *_: (0, 0, 0, 0)) for v in extra],
-            out_specs=pl.BlockSpec(shape, lambda k, *_: (0, 0, 0)),
-            scratch_shapes=[pltpu.VMEM((depth, total), jnp.bfloat16), pltpu.VMEM((total, 8), jnp.int32)],
-        ),
-        out_shape=jax.ShapeDtypeStruct(shape, jnp.bfloat16),
-        cost_estimate=cost(5),
+        in_specs=[smem] * 4 + [pl.BlockSpec(memory_space=pltpu.HBM), vmem] + [vmem] * len(extra),
+        out_specs=vmem,
+        out_shape=jax.ShapeDtypeStruct((count, depth // 2, 2 * NARROW), jnp.bfloat16),
+        scratch_shapes=[
+            pltpu.VMEM((depth, total), jnp.bfloat16),
+            pltpu.VMEM((total, 8), jnp.int32),
+            pltpu.VMEM(integrals.shape, jnp.bfloat16),
+            pltpu.SemaphoreType.DMA((occ_share // K_STEP,)),
+        ],
+        cost_estimate=cost(4),
         compiler_params=pltpu.CompilerParams(vmem_limit_bytes=16 * 1024 * 1024),
     )(occ_irrep, vir_irrep, screen.T, place, integrals, vir_irrep[None, :], *extra)
 
@@ -336,8 +347,9 @@
                 else:
                     far_ref[group, :, pl.ds(pl.multiple_of(j * share, share), share)] = piece
                 folded = piece if folded is None else folded + piece
-            fold_ref[group, :, pl.ds(pl.multiple_of(j * share, share), share)] = folded
-            if few_lhs_ref is not None:
+            if fold_ref is not None:
+                fold_ref[group, :, pl.ds(pl.multiple_of(j * share, share), share)] = folded
+            else:
                 posx = posx_ref[group * K_STEP + j]
 
                 @pl.when((posx >= 0) & (posx < few_lhs_ref.shape[0]))
@@ -345,6 +357,7 @@
                     third = lhs_ref[group, :, pl.ds(pl.multiple_of((2 * K_STEP + j) * share, share), share)]
                     few_lhs_ref[posx, 0] = third
                     few_lhs_ref[posx, 1] = far_ref[group, :, pl.ds(pl.multiple_of(j * share, share), share)]
+                    few_lhs_ref[posx, 2] = folded
 
 
 def masked_amplitudes(amplitudes, occ_irrep, vir_irrep, place, posx, few):
@@ -353,11 +366,11 @@
     smem = pl.BlockSpec(memory_space=pltpu.SMEM)
     vmem = pl.BlockSpec(memory_space=pltpu.VMEM)
     hbm = pl.BlockSpec(memory_space=pltpu.HBM)
-    shapes = [(groups, rows, w) for w in (NEAR * K_STEP * share, K_STEP * share, K_STEP * share)]
-    shapes += [(few, 2, rows, share)] if few else []
+    shapes = [(groups, rows, w) for w in (NEAR * K_STEP * share, K_STEP * share)]
+    shapes += [(few, 3, rows, share)] if few else [(groups, rows, K_STEP * share)]
 
     def kernel(*refs):
-        mask_kernel(*(refs if few else refs[:8] + (None,) + refs[8:]))
+        mask_kernel(*(refs[:7] + (None,) + refs[7:] if few else refs[:8] + (None,) + refs[8:]))
 
     return pl.pallas_call(
         kernel,
@@ -446,35 +459,24 @@
 def make_last_kernel(few, n2, starts2, n3, starts3):
     def kernel(
         occ_ref, vir_ref, pos2_ref, pos3_ref, count_ref, place_ref, fold_ref, far_ref, row_ref, narrow_ref, wide_ref,
-        *refs
+        *refs,
     ):
         m2_refs, refs = refs[:n2], refs[n2:]
         m3_refs = [refs[2 * n:2 * n + 2] for n in range(n3)]
         refs = refs[2 * n3:]
         outs = refs[:4]
-        column_ref, total_ref, short_rhs, far_rhs = refs[4:]
+        column_ref, total_ref, narrow_sum, short_rhs, far_rhs = refs[4:]
         row, col = place_ref[0], place_ref[1]
         at_end = (row == 0) | (row == 3)
-        groups, rows, width = fold_ref.shape
+        groups, rows, width = far_ref.shape if few else fold_ref.shape
         share = width // K_STEP
         batch = rows // share
         @pl.loop(0, groups * K_STEP)
         def _(k):
             here = pl.ds(pl.multiple_of(k * share, share), share)
-            if few:
-                pos2 = pos2_ref[k]
-                at = jnp.maximum(pos2, 0)
-                own, e1, o1, two, three, _ = m2_refs
-                pieces = []
-                for piece in range(2):
-                    close = groups * K_STEP + 2 * at + piece
-                    block = own[at, 1 + piece] + e1[close] + two[at, 1 + piece]
-                    block = block + jnp.where(at_end, three[at, 1 + piece], o1[close])
-                    pieces.append(jnp.where(pos2 >= 0, block, jnp.zeros_like(block)))
-                short = jnp.concatenate(pieces, axis=1)
-            else:
+            if not few:
                 short = chosen(m2_refs, starts2, pos2_ref[k], lambda ref, at: ref[at])
-            short_rhs[here] = jnp.concatenate([short, short], axis=0)
+                short_rhs[here] = jnp.concatenate([short, short], axis=0)
             if n3:
                 far_rhs[here] = chosen(
                     m3_refs, starts3, pos3_ref[k], lambda pair, at: jnp.where(at_end, pair[0][at], pair[1][at])
@@ -482,27 +484,41 @@
 
         column = amplitude_rows(column_ref, row_ref, occ_ref, row, batch, share)
         target = jnp.bitwise_xor(column, occ_ref[batch])
-        both = narrow_ref[...]
         if few:
-            two, three, few_lhs_ref = m2_refs[3:]
+            own, e1, o1, two, three = m2_refs
             half = share // 2
             lane = lax.broadcasted_iota(jnp.int32, (half, 2 * NARROW), 1)
-            for n in range(few_lhs_ref.shape[0]):
-                used = n < count_ref[0]
-                for slot, wanted, ref in ((0, used & at_end, three), (1, used, two)):
+            total_ref[...] = wide_ref[...]
+            narrow_sum[...] = narrow_ref[...]
+
+            @pl.loop(0, count_ref[0])
+            def _(n):
+                for slot, wanted, ref in ((0, at_end, three), (1, True, two)):
                     block = ref[n, 0]
                     zero = jnp.zeros_like(block)
                     block = jnp.where(wanted, block, zero)
                     rhs = jnp.concatenate(
                         [jnp.where(lane < NARROW, block, zero), jnp.where(lane < NARROW, zero, block)], axis=0
                     )
-                    both += jnp.dot(few_lhs_ref[n, slot], rhs, preferred_element_type=jnp.float32)
+                    narrow_sum[...] += jnp.dot(fold_ref[n, slot], rhs, preferred_element_type=jnp.float32)
+                pieces = []
+                for piece in range(2):
+                    close = groups * K_STEP + 2 * n + piece
+                    block = own[n, 1 + piece] + e1[close] + two[n, 1 + piece]
+                    pieces.append(block + jnp.where(at_end, three[n, 1 + piece], o1[close]))
+                short = jnp.concatenate(pieces, axis=1)
+                rhs = jnp.concatenate([short, short], axis=0)
+                total_ref[...] += jnp.dot(fold_ref[n, 2], rhs, preferred_element_type=jnp.float32)
+
+            part, both = total_ref[...], narrow_sum[...]
+        else:
+            part, both = wide_ref[...] if n3 else 0.0, narrow_ref[...]
         both = both + pltpu.roll(both, NARROW, 1)
         both = jnp.concatenate([both] * (FOLD // (2 * NARROW)), axis=1)
-        part = wide_ref[...] if n3 else 0.0
         for group in range(groups):
             here = pl.ds(group * width, width)
-            part += jnp.dot(fold_ref[group], short_rhs[here], preferred_element_type=jnp.float32)
+            if not few:
+                part += jnp.dot(fold_ref[group], short_rhs[here], preferred_element_type=jnp.float32)
             if n3:
                 part += jnp.dot(far_ref[group], far_rhs[here], preferred_element_type=jnp.float32)
         total_ref[...] = jnp.where(target == largest_irrep(vir_ref), part, both)
@@ -512,7 +528,7 @@
 
 
 def last_product(far_lhs, fold, occ_irrep, vir_irrep, pos2, pos3, count, place, narrow_sum, wide_sum, few, m2, m3, batch):
-    groups, rows, width = fold.shape
+    groups, rows, width = far_lhs.shape
     share = rows // batch
     vmem = pl.BlockSpec(memory_space=pltpu.VMEM)
     smem = pl.BlockSpec(memory_space=pltpu.SMEM)
@@ -528,7 +544,8 @@
         scratch_shapes=[
             pltpu.VMEM((vir_irrep.shape[0], 8), jnp.int32),
             pltpu.VMEM((rows, FOLD), jnp.float32),
-            pltpu.VMEM((whole, FOLD), jnp.bfloat16),
+            pltpu.VMEM((rows, 2 * NARROW), jnp.float32),
+            pltpu.VMEM((16 if few else whole, FOLD), jnp.bfloat16),
             pltpu.VMEM((whole if m3 else 16, FOLD), jnp.bfloat16),
         ],
         cost_estimate=cost(4 if m3 else 2),
@@ -593,13 +610,13 @@
             narrow = narrow_blocks(integrals, occ_irrep, vir_irrep, screen, place, few, batch)
             if use_few:
                 e1, o1 = move(narrow, outer), move(narrow, inner)
-                lhs, far_lhs, fold, few_lhs = masked_amplitudes(
+                lhs, far_lhs, fold = masked_amplitudes(
                     amplitudes, occ_irrep, vir_irrep, place, posx, use_few
                 )
                 near, e1, o1, few, _ = lax.optimization_barrier((near, e1, o1, few, fold))
                 two, three = move(few, second), move(few, ends)
                 blocks = (narrow, e1, o1)
-                sums = (few, e1, o1, two, three, few_lhs)
+                sums = (few, e1, o1, two, three)
             else:
                 h1 = [move(v, inward) for v in shorts]
                 o1, e1 = move(narrow, inner), move(narrow, outward)

time: 113 us -> 120 us (1.062)
  the two profiles are of different devices: /device:TPU:6 before, /device:TPU:2 now
where the time goes in v1:
time: 120 us; the launch traced here: 119 us
  waiting for transfers between devices  45.6 us (38%)
  starting transfers between devices  42.1 us (35%)
  Pallas kernels  25.1 us (21%)
  other arithmetic  3.29 us (3%)
  local copies, waits for them, and re-layouts  1.8 us (2%)
    ppermute x9, waiting for transfers between devices, move(): return lax.ppermute(v, 'row', pairs)  35.5 us
    ppermute x3, starting transfers between devices, on_square(): lax.ppermute(quarters[t], 'col', [(q, q ^ t) for q in range(4)])  19.6 us
    ppermute x9, starting transfers between devices, move(): return lax.ppermute(v, 'row', pairs)  16.8 us
    pallas_call x1, Pallas kernels, masked_amplitudes(): pl.pallas_call(kernel, in_specs=[smem, smem, smem, hbm, vmem], out_specs=...  9.15 us
    pallas_call x1, Pallas kernels, first_product(): pl.pallas_call(make_first_kernel(few, len(m3), starts_of([v[0] for v in m...  5.58 us
    ppermute x1, starting transfers between devices, on_square(): lax.ppermute(mine, ('row', 'col'), [(r * 4 + q, q * 4 + r) for r, q in pl...  4.83 us
    pallas_call x1, Pallas kernels, wide_blocks(): pl.pallas_call(kernel, in_specs=[smem] * 4 + [pl.BlockSpec(memory_space=p...  4.56 us
    ppermute x1, waiting for transfers between devices, on_square(): lax.ppermute(mine, ('row', 'col'), [(r * 4 + q, (q ^ 2) * 4 + r) for r, q...  4.07 us
  transfers between devices with their start and end apart: 14, of which 8 were waited for; matrix products, arithmetic and copies ran while one was open for 3% of the time, Pallas kernels for 10%

profile of v1, /device:TPU:2, one launch (start us, length us, event | category | flops | bytes accessed | tf_op | source)
XLA Modules:
  0.0 119.3 jit_solution(10781431058723379702)
XLA Ops:
  0.0 0.1 pad_add_fusion.refs_3_
  0.1 4.6 %shard_map.73 = (bf16[10,3,64,128]{3,2,1,0:T(8,128)(2,1)S(1)}, bf16[22,64,256]{2,1,0:T(8,128)(2,1)S(1)}, bf16[3,64,256]{2,1,0:T(8,128)(2,1)S(1)}, bf16[22,128,25...) custom-call(s32[100]{0:T(128)} %refs_0_.1, ...), custom_call_target="tpu_custom_call" | custom-call | flops 5000000000 | bytes 15000000 | tf_op jit(solution)/shard_map/pallas_call | solution.py:196
  5.3 0.0 copy-start.5
  5.3 0.0 copy-start.3
  5.3 74.4 %conditional.1 = (f32[2,128,128]{2,1,0:T(8,128)S(1)}, f32[2,128,128]{2,1,0:T(8,128)S(1)}, f32[2,128,128]{2,1,0:T(8,128)S(1)}, f32[2,128,128]{1,0,2:T(2,128)S(1)}) conditional(s32[]{:T(128)} %bitcast.21, (s32[512]{0:T(512)S(1)}, s32[100]{0:T(128)S(1)}, s32[2]{0:T(128)S(1)}, s32[25]{0:T(128)S(1)}, ...), branch_computations={%region_0.0_spmd, %region_1.0_spmd, %region_2.0_spmd, %region_3.0_... | conditional | flops 24001843200 | bytes 127558976 | solution.py:671
  5.3 3.5 %collective-permute-start.20 = (bf16[22,64,256]{2,1,0:T(8,128)(2,1)S(1)}, bf16[22,64,256]{2,1,0:T(8,128)(2,1)S(1)}, u32[]{:S(2)}, u32[]{:S(2)}) collective-permute-start(bf16[22,64,256]{2,1,0:T(8,128)(2,1)S(1)} %get-tuple-element.180), channel_id=1, source_target_pairs={{0,4},{12,8},{1,5},{13,9},{2,6},{14,10},{3,7},{15,11},{16,20},{28,... | collective-permute-start | bytes 2162696 | tf_op jit(solution)/shard_map/cond/branch_0_fun/ppermute | solution.py:603
  8.9 3.0 %branch_0_fun.5.refs_0_ = bf16[25,64,128]{2,1,0:T(8,128)(2,1)S(1)} custom-call(s32[100]{0:T(128)S(1)} %get-tuple-element.167.refs_0_.occ_ref, s32[512]{0:T(512)S(1)} %get-tuple-element.168.refs_1_.vir_ref, s32[8,100]{1,0:T(8,128)S(1)} %bitcast.74, s32[2]{0:T(128)S(1)} %get-tuple-element.172.refs_1_.refs_3_.place_ref, ...), custom_call_target="tpu_custom_call" | custom-call | flops 4000000000 | bytes 12000000 | tf_op jit(solution)/shard_map/cond/branch_0_fun/pallas_call | solution.py:250
  11.9 0.7 collective-permute-start.21
  12.5 1.3 %collective-permute-start.22 = (bf16[25,64,128]{2,1,0:T(8,128)(2,1)S(1)}, bf16[25,64,128]{2,1,0:T(8,128)(2,1)S(1)}, u32[]{:S(2)}, u32[]{:S(2)}) collective-permute-start(bf16[25,64,128]{2,1,0:T(8,128)(2,1)S(1)} %branch_0_fun.5.refs_0_), channel_id=1, source_target_pairs={{4,0},{8,12},{5,1},{9,13},{6,2},{10,14},{7,3},{11,15},{20,16},{24,... | collective-permute-start | bytes 1228808 | tf_op jit(solution)/shard_map/cond/branch_0_fun/ppermute | solution.py:603
  13.8 9.1 %branch_0_fun.4 = (bf16[5,512,1920]{2,1,0:T(8,128)(2,1)S(1)}, bf16[5,512,640]{2,1,0:T(8,128)(2,1)S(1)}, bf16[5,512,640]{2,1,0:T(8,128)(2,1)S(1)}) custom-call(s32[100]{0:T(128)S(1)} %get-tuple-element.167.refs_0_.occ_ref, s32[2]{0:T(128)S(1)} %get-tuple-element.172.refs_1_.refs_3_.place_ref, s32[25]{0:T(128)S(1)} %get-tuple-element.173.refs_2_.posx_ref, ...), custom_call_target="tpu_custom_call" | custom-call | flops 7000000000 | bytes 21000000 | tf_op jit(solution)/shard_map/cond/branch_0_fun/pallas_call | solution.py:375
  23.0 2.4 %collective-permute-done.22 = bf16[25,64,128]{2,1,0:T(8,128)(2,1)S(1)} collective-permute-done((bf16[25,64,128]{2,1,0:T(8,128)(2,1)S(1)}, bf16[25,64,128]{2,1,0:T(8,128)(2,1)S(1)}, u32[]{:S(2)}, u32[]{:S(2)}) %collective-permute-start.22) | collective-permute-done | bytes 409632 | tf_op jit(solution)/shard_map/cond/branch_0_fun/ppermute | solution.py:603
  25.4 0.2 add.123
  25.7 0.7 collective-permute-start.23
  26.4 6.0 %collective-permute-start.24 = (bf16[25,64,128]{2,1,0:T(8,128)(2,1)S(1)}, bf16[25,64,128]{2,1,0:T(8,128)(2,1)S(1)}, u32[]{:S(2)}, u32[]{:S(2)}) collective-permute-start(bf16[25,64,128]{2,1,0:T(8,128)(2,1)S(1)} %branch_0_fun.5.refs_0_), channel_id=1, source_target_pairs={{0,4},{12,8},{1,5},{13,9},{2,6},{14,10},{3,7},{15,11},{16,20},{28,... | collective-permute-start | bytes 1228808 | tf_op jit(solution)/shard_map/cond/branch_0_fun/ppermute | solution.py:603
  32.4 1.3 %collective-permute-start.25 = (bf16[25,64,128]{2,1,0:T(8,128)(2,1)S(1)}, bf16[25,64,128]{2,1,0:T(8,128)(2,1)S(1)}, u32[]{:S(2)}, u32[]{:S(2)}) collective-permute-start(bf16[25,64,128]{2,1,0:T(8,128)(2,1)S(1)} %collective-permute-done.21.refs_2_), channel_id=1, source_target_pairs={{4,0},{8,12},{5,1},{9,13},{6,2},{10,14},{7,3},{11,15},{20,16},{24,... | collective-permute-start | bytes 1228808 | tf_op jit(solution)/shard_map/cond/branch_0_fun/ppermute | solution.py:603
  33.7 6.3 %collective-permute-done.24 = bf16[25,64,128]{2,1,0:T(8,128)(2,1)S(1)} collective-permute-done((bf16[25,64,128]{2,1,0:T(8,128)(2,1)S(1)}, bf16[25,64,128]{2,1,0:T(8,128)(2,1)S(1)}, u32[]{:S(2)}, u32[]{:S(2)}) %collective-permute-start.24) | collective-permute-done | bytes 409632 | tf_op jit(solution)/shard_map/cond/branch_0_fun/ppermute | solution.py:603
  40.0 0.1 add.124.refs_1_
  40.1 4.0 %collective-permute-done.25.refs_3_ = bf16[25,64,128]{2,1,0:T(8,128)(2,1)S(1)} collective-permute-done((bf16[25,64,128]{2,1,0:T(8,128)(2,1)S(1)}, bf16[25,64,128]{2,1,0:T(8,128)(2,1)S(1)}, u32[]{:S(2)}, u32[]{:S(2)}) %collective-permute-start.25) | collective-permute-done | bytes 409632 | tf_op jit(solution)/shard_map/cond/branch_0_fun/ppermute | solution.py:603
  44.1 0.2 add.126
  44.4 1.3 %collective-permute-start.28 = (bf16[22,64,256]{2,1,0:T(8,128)(2,1)S(1)}, bf16[22,64,256]{2,1,0:T(8,128)(2,1)S(1)}, u32[]{:S(2)}, u32[]{:S(2)}) collective-permute-start(bf16[22,64,256]{2,1,0:T(8,128)(2,1)S(1)} %add.126), channel_id=1, source_target_pairs={{4,0},{8,12},{5,1},{9,13},{6,2},{10,14},{7,3},{11,15},{20,16},{24,... | collective-permute-start | bytes 2162696 | tf_op jit(solution)/shard_map/cond/branch_0_fun/ppermute | solution.py:603
  45.7 0.7 collective-permute-start.26
  46.4 1.3 %collective-permute-start.27 = (bf16[25,64,128]{2,1,0:T(8,128)(2,1)S(1)}, bf16[25,64,128]{2,1,0:T(8,128)(2,1)S(1)}, u32[]{:S(2)}, u32[]{:S(2)}) collective-permute-start(bf16[25,64,128]{2,1,0:T(8,128)(2,1)S(1)} %collective-permute-done.26.refs_4_), channel_id=1, source_target_pairs={{4,0},{8,12},{5,1},{9,13},{6,2},{10,14},{7,3},{11,15},{20,16},{24,... | collective-permute-start | bytes 1228808 | tf_op jit(solution)/shard_map/cond/branch_0_fun/ppermute | solution.py:603
  47.7 17.7 %collective-permute-done.28 = bf16[22,64,256]{2,1,0:T(8,128)(2,1)S(1)} collective-permute-done((bf16[22,64,256]{2,1,0:T(8,128)(2,1)S(1)}, bf16[22,64,256]{2,1,0:T(8,128)(2,1)S(1)}, u32[]{:S(2)}, u32[]{:S(2)}) %collective-permute-start.28) | collective-permute-done | bytes 720928 | tf_op jit(solution)/shard_map/cond/branch_0_fun/ppermute | solution.py:603
  65.3 0.1 add_add_fusion.refs_0_
  65.4 5.2 %collective-permute-done.27.refs_5_ = bf16[25,64,128]{2,1,0:T(8,128)(2,1)S(1)} collective-permute-done((bf16[25,64,128]{2,1,0:T(8,128)(2,1)S(1)}, bf16[25,64,128]{2,1,0:T(8,128)(2,1)S(1)}, u32[]{:S(2)}, u32[]{:S(2)}) %collective-permute-start.27) | collective-permute-done | bytes 409632 | tf_op jit(solution)/shard_map/cond/branch_0_fun/ppermute | solution.py:603
  70.6 5.6 %branch_0_fun.6 = (f32[512,128]{1,0:T(8,128)S(1)}, f32[16,256]{1,0:T(8,128)S(1)}) custom-call(s32[25]{0:T(128)S(1)} %get-tuple-element.170.pos3_ref, s32[25]{0:T(128)S(1)} %get-tuple-element.173.refs_2_.posx_ref, s32[2]{0:T(128)S(1)} %get-tuple-element.172.refs_1_.refs_3_.place_ref, bf16[5,512,1920]{2,1,0:T(8,128)(2,1)S(1)} %get-tuple-element.176.lhs_ref, ...), custom_call_target="tpu_custom_call" | custom-call | flops 6000000000 | bytes 18000000 | tf_op jit(solution)/shard_map/cond/branch_0_fun/pallas_call | solution.py:445
  76.2 2.8 %branch_0_fun.7 = (f32[2,128,128]{2,1,0:T(8,128)S(1)}, f32[2,128,128]{2,1,0:T(8,128)S(1)}, f32[2,128,128]{2,1,0:T(8,128)S(1)}, f32[2,128,128]{2,1,0:T(8,128)S(1)}) custom-call(s32[100]{0:T(128)S(1)} %get-tuple-element.167.refs_0_.occ_ref, s32[512]{0:T(512)S(1)} %get-tuple-element.168.refs_1_.vir_ref, s32[25]{0:T(128)S(1)} %get-tuple-element.169.pos2_ref, ...), custom_call_target="tpu_custom_call" | custom-call | flops 2000000000 | bytes 6000000 | tf_op jit(solution)/shard_map/cond/branch_0_fun/pallas_call | solution.py:539
  79.0 0.1 copy.19
  79.7 0.1 copy.17
  79.8 3.1 %collective-permute-start.79 = (f32[2,128,128]{1,0,2:T(2,128)S(1)}, f32[2,128,128]{1,0,2:T(2,128)S(1)}, u32[]{:S(2)}, u32[]{:S(2)}) collective-permute-start(f32[2,128,128]{1,0,2:T(2,128)S(1)} %copy.17), channel_id=1, source_target_pairs={{0,3},{1,2},{2,1},{3,0},{4,7},{5,6},{6,5},{7,4},{8,11},{9,10},{10,... | collective-permute-start | bytes 393224 | tf_op jit(solution)/shard_map/ppermute | solution.py:674
  82.9 0.1 copy.16
  83.0 16.4 %collective-permute-start.78 = (f32[2,128,128]{1,0,2:T(2,128)S(1)}, f32[2,128,128]{1,0,2:T(2,128)S(1)}, u32[]{:S(2)}, u32[]{:S(2)}) collective-permute-start(f32[2,128,128]{1,0,2:T(2,128)S(1)} %copy.16), channel_id=1, source_target_pairs={{0,2},{1,3},{2,0},{3,1},{4,6},{5,7},{6,4},{7,5},{8,10},{9,11},{10,... | collective-permute-start | bytes 393224 | tf_op jit(solution)/shard_map/ppermute | solution.py:674
  99.4 0.1 copy.14
  99.5 0.2 collective-permute-start.77
  99.7 0.6 slice.31
  100.3 0.6 slice.33
  100.8 0.6 slice_add_fusion.1
  101.5 0.1 fusion.13
  101.6 0.1 broadcast_subtract_fusion
  101.7 0.6 slice_xor_fusion
  102.3 0.1 fusion.12
  102.4 2.6 %collective-permute-done.78 = f32[2,128,128]{1,0,2:T(2,128)S(1)} collective-permute-done((f32[2,128,128]{1,0,2:T(2,128)S(1)}, f32[2,128,128]{1,0,2:T(2,128)S(1)}, u32[]{:S(2)}, u32[]{:S(2)}) %collective-permute-start.78) | collective-permute-done | bytes 131104 | tf_op jit(solution)/shard_map/ppermute | solution.py:674
  105.0 0.8 collective-permute-start.80
  105.8 4.8 %collective-permute-start.81 = (f32[2,128,128]{1,0,2:T(2,128)S(1)}, f32[2,128,128]{1,0,2:T(2,128)S(1)}, u32[]{:S(2)}, u32[]{:S(2)}) collective-permute-start(f32[2,128,128]{1,0,2:T(2,128)S(1)} %bitcast.51), channel_id=1, source_target_pairs={{0,0},{1,4},{2,8},{3,12},{4,1},{5,5},{6,9},{7,13},{8,2},{9,6},{10,... | collective-permute-start | bytes 393224 | tf_op jit(solution)/shard_map/ppermute | solution.py:676
  110.6 0.1 broadcast_xor_fusion.2
  110.7 4.1 %collective-permute-done.80 = f32[2,128,128]{1,0,2:T(2,128)S(1)} collective-permute-done((f32[2,128,128]{1,0,2:T(2,128)S(1)}, f32[2,128,128]{1,0,2:T(2,128)S(1)}, u32[]{:S(2)}, u32[]{:S(2)}) %collective-permute-start.80) | collective-permute-done | bytes 131104 | tf_op jit(solution)/shard_map/ppermute | solution.py:677
  114.8 3.5 %collective-permute-done.81 = f32[2,128,128]{1,0,2:T(2,128)S(1)} collective-permute-done((f32[2,128,128]{1,0,2:T(2,128)S(1)}, f32[2,128,128]{1,0,2:T(2,128)S(1)}, u32[]{:S(2)}, u32[]{:S(2)}) %collective-permute-start.81) | collective-permute-done | bytes 131104 | tf_op jit(solution)/shard_map/ppermute | solution.py:676
  118.3 1.0 fusion.11
  (17 shorter events, 0.1 us)
Async XLA Ops:
  0.1 5.2 %copy-start.1 = (s32[512]{0:T(512)S(1)}, s32[512]{0:T(512)}, u32[]{:S(2)}) copy-start(s32[512]{0:T(512)} %refs_1_.1) | copy-start | bytes 6148
  0.1 5.2 %copy-start.2 = (s32[100,8]{0,1:T(8,128)S(1)}, s32[100,8]{0,1:T(8,128)}, u32[]{:S(2)}) copy-start(s32[100,8]{0,1:T(8,128)} %param.18) | copy-start | bytes 9604
  0.1 5.2 %copy-start.4 = (s32[100]{0:T(128)S(1)}, s32[100]{0:T(128)}, u32[]{:S(2)}) copy-start(s32[100]{0:T(128)} %refs_0_.1) | copy-start | bytes 1204
  5.3 95.0 %copy-start.5 = (f32[100]{0:T(128)S(1)}, f32[100]{0:T(128)}, u32[]{:S(2)}) copy-start(f32[100]{0:T(128)} %param.19) | copy-start | bytes 1204
  5.3 96.2 %copy-start.3 = (f32[512]{0:T(512)S(1)}, f32[512]{0:T(512)}, u32[]{:S(2)}) copy-start(f32[512]{0:T(512)} %param.20) | copy-start | bytes 6148
  5.3 20.1 %collective-permute-start.20 = (bf16[22,64,256]{2,1,0:T(8,128)(2,1)S(1)}, bf16[22,64,256]{2,1,0:T(8,128)(2,1)S(1)}, u32[]{:S(2)}, u32[]{:S(2)}) collective-permute-start(bf16[22,64,256]{2,1,0:T(8,128)(2,1)S(1)} %get-tuple-element.180), channel_id=1, source_target_pairs={{0,4},{12,8},{1,5},{13,9},{2,6},{14,10},{3,7},{15,11},{16,20},{28,... | collective-permute-start | bytes 2162696 | tf_op jit(solution)/shard_map/cond/branch_0_fun/ppermute | solution.py:603
  11.9 11.2 %collective-permute-start.21 = (bf16[25,64,128]{2,1,0:T(8,128)(2,1)S(1)}, bf16[25,64,128]{2,1,0:T(8,128)(2,1)S(1)}, u32[]{:S(2)}, u32[]{:S(2)}) collective-permute-start(bf16[25,64,128]{2,1,0:T(8,128)(2,1)S(1)} %branch_0_fun.5.refs_0_), channel_id=1, source_target_pairs={{4,8},{8,4},{5,9},{9,5},{6,10},{10,6},{7,11},{11,7},{20,24},{24,20... | collective-permute-start | bytes 1228808 | tf_op jit(solution)/shard_map/cond/branch_0_fun/ppermute | solution.py:603
  12.5 12.9 %collective-permute-start.22 = (bf16[25,64,128]{2,1,0:T(8,128)(2,1)S(1)}, bf16[25,64,128]{2,1,0:T(8,128)(2,1)S(1)}, u32[]{:S(2)}, u32[]{:S(2)}) collective-permute-start(bf16[25,64,128]{2,1,0:T(8,128)(2,1)S(1)} %branch_0_fun.5.refs_0_), channel_id=1, source_target_pairs={{4,0},{8,12},{5,1},{9,13},{6,2},{10,14},{7,3},{11,15},{20,16},{24,... | collective-permute-start | bytes 1228808 | tf_op jit(solution)/shard_map/cond/branch_0_fun/ppermute | solution.py:603
  25.7 18.5 %collective-permute-start.23 = (bf16[22,64,256]{2,1,0:T(8,128)(2,1)S(1)}, bf16[22,64,256]{2,1,0:T(8,128)(2,1)S(1)}, u32[]{:S(2)}, u32[]{:S(2)}) collective-permute-start(bf16[22,64,256]{2,1,0:T(8,128)(2,1)S(1)} %add.123), channel_id=1, source_target_pairs={{4,8},{8,4},{5,9},{9,5},{6,10},{10,6},{7,11},{11,7},{20,24},{24,20... | collective-permute-start | bytes 2162696 | tf_op jit(solution)/shard_map/cond/branch_0_fun/ppermute | solution.py:603
  26.4 13.6 %collective-permute-start.24 = (bf16[25,64,128]{2,1,0:T(8,128)(2,1)S(1)}, bf16[25,64,128]{2,1,0:T(8,128)(2,1)S(1)}, u32[]{:S(2)}, u32[]{:S(2)}) collective-permute-start(bf16[25,64,128]{2,1,0:T(8,128)(2,1)S(1)} %branch_0_fun.5.refs_0_), channel_id=1, source_target_pairs={{0,4},{12,8},{1,5},{13,9},{2,6},{14,10},{3,7},{15,11},{16,20},{28,... | collective-permute-start | bytes 1228808 | tf_op jit(solution)/shard_map/cond/branch_0_fun/ppermute | solution.py:603
  32.4 11.7 %collective-permute-start.25 = (bf16[25,64,128]{2,1,0:T(8,128)(2,1)S(1)}, bf16[25,64,128]{2,1,0:T(8,128)(2,1)S(1)}, u32[]{:S(2)}, u32[]{:S(2)}) collective-permute-start(bf16[25,64,128]{2,1,0:T(8,128)(2,1)S(1)} %collective-permute-done.21.refs_2_), channel_id=1, source_target_pairs={{4,0},{8,12},{5,1},{9,13},{6,2},{10,14},{7,3},{11,15},{20,16},{24,... | collective-permute-start | bytes 1228808 | tf_op jit(solution)/shard_map/cond/branch_0_fun/ppermute | solution.py:603
  44.4 21.0 %collective-permute-start.28 = (bf16[22,64,256]{2,1,0:T(8,128)(2,1)S(1)}, bf16[22,64,256]{2,1,0:T(8,128)(2,1)S(1)}, u32[]{:S(2)}, u32[]{:S(2)}) collective-permute-start(bf16[22,64,256]{2,1,0:T(8,128)(2,1)S(1)} %add.126), channel_id=1, source_target_pairs={{4,0},{8,12},{5,1},{9,13},{6,2},{10,14},{7,3},{11,15},{20,16},{24,... | collective-permute-start | bytes 2162696 | tf_op jit(solution)/shard_map/cond/branch_0_fun/ppermute | solution.py:603
  45.7 0.7 collective-permute-start.26
  46.4 24.2 %collective-permute-start.27 = (bf16[25,64,128]{2,1,0:T(8,128)(2,1)S(1)}, bf16[25,64,128]{2,1,0:T(8,128)(2,1)S(1)}, u32[]{:S(2)}, u32[]{:S(2)}) collective-permute-start(bf16[25,64,128]{2,1,0:T(8,128)(2,1)S(1)} %collective-permute-done.26.refs_4_), channel_id=1, source_target_pairs={{4,0},{8,12},{5,1},{9,13},{6,2},{10,14},{7,3},{11,15},{20,16},{24,... | collective-permute-start | bytes 1228808 | tf_op jit(solution)/shard_map/cond/branch_0_fun/ppermute | solution.py:603
  79.8 22.6 %collective-permute-start.79 = (f32[2,128,128]{1,0,2:T(2,128)S(1)}, f32[2,128,128]{1,0,2:T(2,128)S(1)}, u32[]{:S(2)}, u32[]{:S(2)}) collective-permute-start(f32[2,128,128]{1,0,2:T(2,128)S(1)} %copy.17), channel_id=1, source_target_pairs={{0,3},{1,2},{2,1},{3,0},{4,7},{5,6},{6,5},{7,4},{8,11},{9,10},{10,... | collective-permute-start | bytes 393224 | tf_op jit(solution)/shard_map/ppermute | solution.py:674
  83.0 21.9 %collective-permute-start.78 = (f32[2,128,128]{1,0,2:T(2,128)S(1)}, f32[2,128,128]{1,0,2:T(2,128)S(1)}, u32[]{:S(2)}, u32[]{:S(2)}) collective-permute-start(f32[2,128,128]{1,0,2:T(2,128)S(1)} %copy.16), channel_id=1, source_target_pairs={{0,2},{1,3},{2,0},{3,1},{4,6},{5,7},{6,4},{7,5},{8,10},{9,11},{10,... | collective-permute-start | bytes 393224 | tf_op jit(solution)/shard_map/ppermute | solution.py:674
  99.5 5.4 %collective-permute-start.77 = (f32[2,128,128]{1,0,2:T(2,128)S(1)}, f32[2,128,128]{1,0,2:T(2,128)S(1)}, u32[]{:S(2)}, u32[]{:S(2)}) collective-permute-start(f32[2,128,128]{1,0,2:T(2,128)S(1)} %copy.14), channel_id=1, source_target_pairs={{0,1},{1,0},{2,3},{3,2},{4,5},{5,4},{6,7},{7,6},{8,9},{9,8},{10,11... | collective-permute-start | bytes 393224 | tf_op jit(solution)/shard_map/ppermute | solution.py:674
  105.0 9.8 %collective-permute-start.80 = (f32[2,128,128]{1,0,2:T(2,128)S(1)}, f32[2,128,128]{1,0,2:T(2,128)S(1)}, u32[]{:S(2)}, u32[]{:S(2)}) collective-permute-start(f32[2,128,128]{1,0,2:T(2,128)S(1)} %bitcast.50), channel_id=1, source_target_pairs={{0,8},{1,12},{2,0},{3,4},{4,9},{5,13},{6,1},{7,5},{8,10},{9,14},{1... | collective-permute-start | bytes 393224 | tf_op jit(solution)/shard_map/ppermute | solution.py:677
  105.8 12.4 %collective-permute-start.81 = (f32[2,128,128]{1,0,2:T(2,128)S(1)}, f32[2,128,128]{1,0,2:T(2,128)S(1)}, u32[]{:S(2)}, u32[]{:S(2)}) collective-permute-start(f32[2,128,128]{1,0,2:T(2,128)S(1)} %bitcast.51), channel_id=1, source_target_pairs={{0,0},{1,4},{2,8},{3,12},{4,1},{5,5},{6,9},{7,13},{8,2},{9,6},{10,... | collective-permute-start | bytes 393224 | tf_op jit(solution)/shard_map/ppermute | solution.py:676
